TPU v7x, 32 devices: a whole 2x2x4 slice. The times are simulated.
32 devices in a mesh: rows: 8 (over z, x), filt: 4 (over y, core).
Axes of the slice: x: 2, y: 2, z: 4, core: 2. Of those that a mesh axis runs over, the one named last changes fastest.
Arguments:
- features: bfloat16 [96, 48, 2048], P('rows'), may hold values from -6 to 6
- point_weight: bfloat16 [2048, 256], P(None, 'filt'), may hold values from -0.125 to 0.125
- dilated_weight: bfloat16 [3, 3, 3, 2048, 256], P(None, None, None, None, 'filt'), may hold values from -0.046875 to 0.046875
- branch_bias: float32 [4, 256], P(None, 'filt'), may hold values from -3 to 3
- project_weight: bfloat16 [4, 256, 256], replicated, may hold values from -0.1875 to 0.1875
- project_bias: float32 [256], replicated, may hold values from -3 to 3
- cotangent: bfloat16 [96, 48, 256], P('rows'), may hold values from -6 to 6
Outputs:
- head_output: bfloat16 [96, 48, 256], P('rows', None, 'filt')
- feature_grad: bfloat16 [96, 48, 2048], P('rows', None, 'filt')
All inputs are finite; a program needn't handle non-finite values.
Results may differ from a plain program's by a relative error of at most 0.035.
The roundings to bfloat16 on the way count: a program that leaves them out, or rounds other values in their place, can miss the bound.
Values may be sent and summed in bfloat16 or wider, within the bound.
No kernel may reach another device: no remote copies, remote signals or barrier semaphores. Data moves between devices by JAX's collectives and lax.ppermute only.
A program may use at most 128 MiB of HBM per device.

v0:
```python
import functools

import jax
import jax.numpy as jnp
import numpy as np
from jax import lax
from jax.experimental import pallas as pl
from jax.experimental.pallas import tpu as pltpu
from jax.sharding import PartitionSpec as P

FIRST_DILATION = 12
SECOND_DILATION = 24
THIRD_DILATION = 36


def passed_along(x, axis, by):
    devices = lax.axis_size(axis)
    pairs = [(i, i + by) for i in range(devices) if 0 <= i + by < devices]
    return lax.ppermute(x, axis, pairs)


def shift_columns(field, amount):
    breadth = field.shape[1]
    if amount == 0:
        return field
    padding = [(0, 0)] * field.ndim
    if amount > 0:
        kept = field[:, amount:]
        padding[1] = (0, amount)
    else:
        kept = field[:, : breadth + amount]
        padding[1] = (-amount, 0)
    return jnp.pad(kept, padding)


def fetch_sums(field, offset):
    return passed_along(field, "rows", offset)


def fetch_grads(field, offset):
    return passed_along(field, "rows", offset)


def shift_rows(field, amount, fetcher):
    height = field.shape[0]
    quotient = amount // height

    def extract_block(offset):
        if offset == 0:
            return field
        return fetcher(field, offset)

    return extract_block(quotient)


def make_kernel_taps(variants, dilation_rates):
    stacked = [variants[:, :, 0]]
    for branch, dilation in enumerate(dilation_rates):
        for row_tap in range(3):
            source = variants[:, :, 1 + 3 * branch + row_tap]
            for col_tap in range(3):
                stacked.append(shift_columns(source, -(col_tap - 1) * dilation))
    return jnp.stack(stacked, 2)


def on_device_general(
    features, point_weight, dilated_weight, branch_bias, project_weight, project_bias, cotangent
):
    height, breadth, channels = features.shape
    pixels = height * breadth
    own_width = point_weight.shape[1]
    filters = lax.axis_size("filt")
    member = lax.axis_index("filt")
    branch_outputs = project_weight.shape[2]
    own_out = branch_outputs // filters
    own_channels = channels // filters
    dilation_rates = (FIRST_DILATION, SECOND_DILATION, THIRD_DILATION)
    all_weights = jnp.concatenate(
        [point_weight[None], dilated_weight.reshape(27, channels, own_width)], 0
    )
    flattened = features.reshape(pixels, channels)
    tap_terms = jnp.einsum(
        "pc,tco->pto", flattened, all_weights, preferred_element_type=jnp.float32
    )
    tap_terms = tap_terms.reshape(height, breadth, 28, own_width)
    pre_list = [tap_terms[:, :, 0, :] + branch_bias[0]]
    for branch, dilation in enumerate(dilation_rates):
        summed_result = jnp.zeros((height, breadth, own_width), jnp.float32)
        for row_tap in range(3):
            row_sum = jnp.zeros((height, breadth, own_width), jnp.float32)
            for col_tap in range(3):
                row_sum = row_sum + shift_columns(
                    tap_terms[:, :, 1 + 9 * branch + 3 * row_tap + col_tap, :],
                    (col_tap - 1) * dilation,
                )
            summed_result = summed_result + shift_rows(
                row_sum, -(row_tap - 1) * dilation, fetch_sums
            )
        pre_list.append(summed_result + branch_bias[branch + 1])
    branch_pre = jnp.stack(pre_list, 2)
    activations = jnp.maximum(branch_pre, 0.0).astype(jnp.bfloat16).reshape(pixels, 4 * own_width)
    grouped = project_weight.reshape(4, filters, own_width, branch_outputs)
    own_rows = lax.dynamic_index_in_dim(grouped, member, 1, keepdims=False).reshape(
        4 * own_width, branch_outputs
    )
    flat_cotangent = cotangent.reshape(pixels, branch_outputs)
    ordered = jnp.transpose(grouped, (1, 0, 2, 3)).reshape(filters * 4 * own_width, branch_outputs)
    project_pre = jnp.dot(
        lax.all_gather(activations, "filt", axis=1, tiled=True),
        ordered,
        preferred_element_type=jnp.float32,
    )
    project_pre = project_pre + project_bias
    head_grad = jnp.where(project_pre > 0, flat_cotangent.astype(jnp.float32), 0.0).astype(
        jnp.bfloat16
    )
    own_pre = lax.dynamic_slice_in_dim(project_pre, member * own_out, own_out, 1)
    act_grad = jnp.dot(head_grad, own_rows.T, preferred_element_type=jnp.float32)
    head_output = jnp.maximum(own_pre, 0.0).astype(jnp.bfloat16).reshape(height, breadth, own_out)
    branch_grad = jnp.where(
        branch_pre > 0, act_grad.reshape(height, breadth, 4, own_width), 0.0
    ).astype(jnp.bfloat16)
    variant_list = [branch_grad[:, :, 0, :]]
    for branch, dilation in enumerate(dilation_rates):
        for row_tap in range(3):
            variant_list.append(
                shift_rows(branch_grad[:, :, branch + 1, :], (row_tap - 1) * dilation, fetch_grads)
            )
    variants = jnp.stack(variant_list, 2)
    stacked = make_kernel_taps(variants, dilation_rates).reshape(pixels, 28, own_width)
    input_grad = lax.psum_scatter(
        jnp.einsum("pto,tco->cp", stacked, all_weights, preferred_element_type=jnp.float32),
        "filt",
        scatter_dimension=0,
        tiled=True,
    ).T
    feature_grad = input_grad.astype(jnp.bfloat16).reshape(height, breadth, own_channels)
    return (head_output, feature_grad)


W = 64
BLOCK = 144
PIXELS = 576
HALF = 288
CHANNELS = 2048
F32 = jnp.float32
BF16 = jnp.bfloat16

OUT_PAIRS = ((3, 1), (1, 1), (3, 0), (1, 0), (3, 2), (1, 2), (2, 1), (2, 0), (2, 2))
TAPS = (
    [(k, 1, 1) for k in (1, 2, 3)]
    + [(k, i, j) for k, j in OUT_PAIRS for i in (0, 2)]
    + [(k, 1, j) for j in (0, 2) for k in (1, 2, 3)]
)
ODD_AT, EVEN_AT, LEFT_AT, RIGHT_AT = 4 * W, 16 * W, 22 * W, 25 * W
SWAPS = (5, 7, 3, 1, 6, 2)


def fits(mesh):
    return mesh.shape["rows"] == 8 and mesh.shape["filt"] == 4


def order_matrix():
    to = np.zeros((192, 192), np.float32)
    for m in range(4):
        for r in range(4):
            for c in range(12):
                to[m * 48 + r * 12 + c, r * 48 + m * 12 + c] = 1
    return to


def tap_index(tap):
    k, i, j = tap
    return (k - 1) * 9 + i * 3 + j


def nt(a, b):
    return lax.dot_general(a, b, (((1,), (1,)), ((), ())), preferred_element_type=F32)


def nn(a, b):
    return lax.dot_general(a, b, (((1,), (0,)), ((), ())), preferred_element_type=F32)


def into_blocks(order, read, write):
    for g in range(3):
        moved = nn(order, read(g * 192)).astype(BF16)
        for m in range(4):
            write(m * BLOCK + g * 48, moved[m * 48 : (m + 1) * 48])


def from_blocks(order_t, value, write):
    for g in range(3):
        parts = [value[m * BLOCK + g * 48 : m * BLOCK + g * 48 + 48] for m in range(4)]
        write(g * 192, nn(order_t, jnp.concatenate(parts, 0)).astype(BF16))


def low_lanes(shape):
    return lax.broadcasted_iota(jnp.int32, shape, 1) % 128 < W


def outward_slot(row, x):
    other = row ^ x
    apart = jnp.abs(other - row)
    slot = apart - 1 + jnp.where(other < row, 3, 0)
    return jnp.where(apart <= 3, slot, 0)


def pack_rows(sums, packed, k):
    low = low_lanes((HALF, 128))
    top, bottom = sums[k - 1, :HALF, :], sums[k - 1, HALF:, :]
    packed[k - 1] = jnp.where(low, top, pltpu.roll(bottom, W, 1))
    packed[k + 2] = jnp.where(low, pltpu.roll(top, W, 1), bottom)


def odd_kernel(row_ref, features, dilated, point, order, *refs):
    out, ordered, weights = refs[0:4], refs[4], refs[5]
    raw, sums, packed, feature_sems, weight_sems = refs[6:]
    loads = []
    for g in range(3):
        rows = pl.ds(g * 192, 192)
        loads.append(pltpu.make_async_copy(features.at[rows], raw.at[rows], feature_sems.at[g]))
        loads[-1].start()
    fetches = [pltpu.make_async_copy(point, weights.at[pl.ds(0, W)], weight_sems.at[0])]
    for q, tap in enumerate(TAPS):
        fetches.append(
            pltpu.make_async_copy(
                dilated.at[tap_index(tap)],
                weights.at[pl.ds((q + 1) * W, W)],
                weight_sems.at[q + 1],
            )
        )
    for fetch in fetches[4:] + fetches[:4]:
        fetch.start()
    for g in range(3):
        loads[g].wait()
        moved = nn(order[...], raw[g * 192 : (g + 1) * 192, :]).astype(BF16)
        for m in range(4):
            at = m * BLOCK + g * 48
            ordered[at : at + 48, :] = moved[m * 48 : (m + 1) * 48]

    def product(pair, first, last):
        for fetch in fetches[4 + 2 * pair : 8 + 2 * pair]:
            fetch.wait()
        at = ODD_AT + pair * 128
        return nt(ordered[first * BLOCK : last * BLOCK, :], weights[at : at + 256, :])

    d = product(0, 0, 4)
    sums[2] = d[:, :128]
    sums[0] = d[:, 128:]
    d = product(2, 0, 3)
    sums[2, 3 * BLOCK :, :] = sums[2, 3 * BLOCK :, :] + d[:BLOCK, :128]
    sums[0, BLOCK:, :] = sums[0, BLOCK:, :] + d[:, 128:]
    d = product(4, 1, 4)
    sums[2, :BLOCK, :] = sums[2, :BLOCK, :] + d[2 * BLOCK :, :128]
    sums[0, : 3 * BLOCK, :] = sums[0, : 3 * BLOCK, :] + d[:, 128:]
    pack_rows(sums, packed, 3)
    pack_rows(sums, packed, 1)
    for n in range(4):
        out[n][...] = packed[outward_slot(row_ref[0], SWAPS[n])]
    for fetch in fetches[:4] + fetches[16:]:
        fetch.wait()


def odd_sums(row, features, dilated, point, order):
    return pl.pallas_call(
        odd_kernel,
        out_shape=[jax.ShapeDtypeStruct((HALF, 128), F32)] * 4
        + [pltpu.VMEM((PIXELS, CHANNELS), BF16), pltpu.VMEM((28 * W, CHANNELS), BF16)],
        in_specs=[pl.BlockSpec(memory_space=pltpu.SMEM)]
        + [pl.BlockSpec(memory_space=pltpu.HBM)] * 3
        + [pl.BlockSpec(memory_space=pltpu.VMEM)],
        out_specs=[pl.BlockSpec(memory_space=pltpu.VMEM)] * 6,
        scratch_shapes=[
            pltpu.VMEM((PIXELS, CHANNELS), BF16),
            pltpu.VMEM((3, PIXELS, 128), F32),
            pltpu.VMEM((6, HALF, 128), F32),
            pltpu.SemaphoreType.DMA((3,)),
            pltpu.SemaphoreType.DMA((28,)),
        ],
        compiler_params=pltpu.CompilerParams(vmem_limit_bytes=28 * 2**20),
        name="odd_sums",
    )(row, features, dilated, point, order)


def even_kernel(row_ref, ordered, weights, *refs):
    out = refs[0:2]
    sums, packed = refs[2:]
    d = nt(ordered[...], weights[EVEN_AT : EVEN_AT + 384, :])
    sums[1] = d[:, :128]
    sums[1, 2 * BLOCK :, :] = sums[1, 2 * BLOCK :, :] + d[: 2 * BLOCK, 128:256]
    sums[1, : 2 * BLOCK, :] = sums[1, : 2 * BLOCK, :] + d[2 * BLOCK :, 256:]
    pack_rows(sums, packed, 2)
    for n in range(2):
        slot = jnp.where((row_ref[0] ^ SWAPS[4 + n]) < row_ref[0], 4, 1)
        out[n][...] = packed[slot]


def even_sums(row, ordered, weights):
    return pl.pallas_call(
        even_kernel,
        out_shape=[jax.ShapeDtypeStruct((HALF, 128), F32)] * 2,
        in_specs=[
            pl.BlockSpec(memory_space=pltpu.SMEM),
            pl.BlockSpec(memory_space=pltpu.VMEM),
            pl.BlockSpec(memory_space=pltpu.VMEM),
        ],
        out_specs=[pl.BlockSpec(memory_space=pltpu.VMEM)] * 2,
        scratch_shapes=[
            pltpu.VMEM((3, PIXELS, 128), F32),
            pltpu.VMEM((6, HALF, 128), F32),
        ],
        compiler_params=pltpu.CompilerParams(vmem_limit_bytes=18 * 2**20),
        cost_estimate=pl.CostEstimate(flops=10**6, bytes_accessed=10**4, transcendentals=0),
        name="even_sums",
    )(row, ordered, weights)


def own_kernel(ordered, weights, bias, out):
    out[...] = nt(ordered[...], weights[:256, :]) + bias[...]
    low = low_lanes((PIXELS, 128))

    def add(first, value, k):
        lanes = slice(0, 128) if k == 1 else slice(128, 256)
        rows = slice(first * BLOCK, first * BLOCK + value.shape[0])
        mask = low[: value.shape[0]]
        kept = jnp.where(mask, value[:, lanes], 0.0) if k == 2 else jnp.where(mask, 0.0, value[:, lanes])
        out[rows, lanes] = out[rows, lanes] + kept

    d = nt(ordered[: 3 * BLOCK, :], weights[LEFT_AT - W : LEFT_AT + 3 * W, :])
    for k in (1, 2, 3):
        add(k, d[: (4 - k) * BLOCK], k)
    d = nt(ordered[BLOCK:, :], weights[RIGHT_AT - W : RIGHT_AT + 3 * W, :])
    for k in (1, 2, 3):
        add(0, d[(k - 1) * BLOCK :], k)


def own_sums(ordered, weights, bias):
    return pl.pallas_call(
        own_kernel,
        out_shape=jax.ShapeDtypeStruct((PIXELS, 4 * W), F32),
        in_specs=[pl.BlockSpec(memory_space=pltpu.VMEM)] * 3,
        out_specs=pl.BlockSpec(memory_space=pltpu.VMEM),
        compiler_params=pltpu.CompilerParams(vmem_limit_bytes=18 * 2**20),
        cost_estimate=pl.CostEstimate(flops=10**6, bytes_accessed=10**4, transcendentals=0),
        name="own_sums",
    )(ordered, weights, bias)


def arrival_slot(row, other):
    return jnp.where((other >= 0) & (other < 8), row ^ other, 0)


def gather_arrivals(recv, arrivals):
    arrivals[0] = jnp.zeros((HALF, 128), arrivals.dtype)
    for n, x in enumerate(SWAPS):
        arrivals[x] = recv[n][...]


def activation_kernel(row_ref, own, *refs):
    recv, acts, arrivals = refs[:6], refs[6], refs[7]
    row = row_ref[0]
    gather_arrivals(recv, arrivals)
    low = low_lanes((HALF, 128))
    t1, t2, t3 = (
        arrivals[arrival_slot(row, row - k)] + arrivals[arrival_slot(row, row + k)]
        for k in (1, 2, 3)
    )
    r1, r2, r3 = (pltpu.roll(t, W, 1) for t in (t1, t2, t3))
    for rows, a, b, c in ((slice(0, HALF), r1, t2, r3), (slice(HALF, PIXELS), t1, r2, t3)):
        left = own[rows, :128] + jnp.where(low, 0.0, a)
        right = own[rows, 128:] + jnp.where(low, b, c)
        acts[rows, :128] = jnp.maximum(left, 0.0).astype(BF16)
        acts[rows, 128:] = jnp.maximum(right, 0.0).astype(BF16)


def activations_of(row, own, received):
    return pl.pallas_call(
        activation_kernel,
        out_shape=jax.ShapeDtypeStruct((PIXELS, 4 * W), BF16),
        in_specs=[pl.BlockSpec(memory_space=pltpu.SMEM)]
        + [pl.BlockSpec(memory_space=pltpu.VMEM)] * 7,
        out_specs=pl.BlockSpec(memory_space=pltpu.VMEM),
        scratch_shapes=[pltpu.VMEM((8, HALF, 128), F32)],
        compiler_params=pltpu.CompilerParams(vmem_limit_bytes=8 * 2**20),
        name="activations",
    )(row, own, *received)


def head_kernel(row_ref, member_ref, a0, a1, a2, a3, project, bias, cotangent, order, order_t, *refs):
    head_out, grads, sends, ordered, packed = refs[0], refs[1], refs[2:8], refs[8], refs[9]
    member = member_ref[0]

    def rows_of(who):
        at = pl.multiple_of(who * W, W)
        return jnp.concatenate([project[k, pl.ds(at, W), :] for k in range(4)], 0)

    own_rows = rows_of(member)
    pre = nn(a0[...], own_rows) + bias[...]
    for flip, acts in ((1, a1), (2, a2), (3, a3)):
        pre = pre + nn(acts[...], rows_of(member ^ flip))
    mine = jnp.zeros((PIXELS, W), F32)
    for q in range(4):
        mine = mine + jnp.where(member == q, pre[:, q * W : (q + 1) * W], 0.0)
    mine = jnp.maximum(mine, 0.0).astype(BF16)

    def put(at, value):
        head_out[at : at + 192, :] = value

    from_blocks(order_t[...], mine, put)
    for g in range(3):
        moved = nn(order[...], cotangent[g * 192 : (g + 1) * 192, :])
        for m in range(4):
            at = m * BLOCK + g * 48
            ordered[at : at + 48, :] = moved[m * 48 : (m + 1) * 48]
    head_grad = jnp.where(pre > 0, ordered[...], 0.0).astype(BF16)
    act_grad = nt(head_grad, own_rows)
    grad = jnp.where(a0[...].astype(F32) > 0, act_grad, 0.0)
    grads[...] = grad.astype(BF16)
    low = low_lanes((HALF, 128))
    left, right = grad[:, :128], grad[:, 128:]
    packed[0] = jnp.where(low, pltpu.roll(left[:HALF], W, 1), left[HALF:]).astype(BF16)
    packed[1] = jnp.where(low, right[:HALF], pltpu.roll(right[HALF:], W, 1)).astype(BF16)
    packed[2] = jnp.where(low, pltpu.roll(right[:HALF], W, 1), right[HALF:]).astype(BF16)
    for n, x in enumerate(SWAPS):
        apart = jnp.abs((row_ref[0] ^ x) - row_ref[0])
        sends[n][...] = packed[jnp.where(apart <= 3, apart - 1, 0)]


def head(row, member, acts, project, bias, cotangent, order, order_t):
    return pl.pallas_call(
        head_kernel,
        out_shape=[
            jax.ShapeDtypeStruct((PIXELS, W), BF16),
            jax.ShapeDtypeStruct((PIXELS, 4 * W), BF16),
        ]
        + [jax.ShapeDtypeStruct((HALF, 128), BF16)] * 6,
        in_specs=[pl.BlockSpec(memory_space=pltpu.SMEM)] * 2
        + [pl.BlockSpec(memory_space=pltpu.VMEM)] * 9,
        out_specs=[pl.BlockSpec(memory_space=pltpu.VMEM)] * 8,
        scratch_shapes=[pltpu.VMEM((PIXELS, 256), F32), pltpu.VMEM((3, HALF, 128), BF16)],
        compiler_params=pltpu.CompilerParams(vmem_limit_bytes=12 * 2**20),
        name="head",
    )(row, member, *acts, project, bias, cotangent, order, order_t)


def spread_kernel(row_ref, own, *refs):
    recv, stack, arrivals, pairs, twice = refs[:6], refs[6], refs[7], refs[8], refs[9]
    row = row_ref[0]
    gather_arrivals(recv, arrivals)
    low = low_lanes((HALF, 128))
    low_all = low_lanes((PIXELS, 128))
    for k in (1, 2, 3):
        p = arrivals[arrival_slot(row, row + k)].astype(F32)
        m = arrivals[arrival_slot(row, row - k)].astype(F32)
        pairs[k - 1, :HALF, :] = jnp.where(low, p, pltpu.roll(m, W, 1)).astype(BF16)
        pairs[k - 1, HALF:, :] = jnp.where(low, pltpu.roll(p, W, 1), m).astype(BF16)
        g = own[:, :128].astype(F32) if k == 1 else own[:, 128:].astype(F32)
        other = pltpu.roll(g, W, 1)
        both = jnp.where(low_all, g, other) if k == 2 else jnp.where(low_all, other, g)
        twice[k - 1] = both.astype(BF16)
    stack[:, : 4 * W] = own[...]
    nothing = jnp.zeros((BLOCK, 128), BF16)

    def block_of(ref, k, source):
        if 0 <= source < 4:
            return ref[k - 1, source * BLOCK : (source + 1) * BLOCK, :]
        return nothing

    for q, (k, j) in enumerate(OUT_PAIRS):
        lanes = slice(ODD_AT + q * 128, ODD_AT + q * 128 + 128)
        for m in range(4):
            stack[m * BLOCK : (m + 1) * BLOCK, lanes] = block_of(pairs, k, m - (j - 1) * k)
    low_block = low_lanes((BLOCK, 128))
    for q, (a, b) in enumerate(((1, 2), (3, -1), (-2, -3))):
        lanes = slice(LEFT_AT + q * 128, LEFT_AT + q * 128 + 128)
        for m in range(4):
            stack[m * BLOCK : (m + 1) * BLOCK, lanes] = jnp.where(
                low_block, block_of(twice, abs(a), m + a), block_of(twice, abs(b), m + b)
            )


def spread(row, own, received):
    return pl.pallas_call(
        spread_kernel,
        out_shape=pltpu.VMEM((PIXELS, 28 * W), BF16),
        in_specs=[pl.BlockSpec(memory_space=pltpu.SMEM)]
        + [pl.BlockSpec(memory_space=pltpu.VMEM)] * 7,
        out_specs=pl.BlockSpec(memory_space=pltpu.VMEM),
        scratch_shapes=[
            pltpu.VMEM((8, HALF, 128), BF16),
            pltpu.VMEM((3, PIXELS, 128), BF16),
            pltpu.VMEM((3, PIXELS, 128), BF16),
        ],
        compiler_params=pltpu.CompilerParams(vmem_limit_bytes=12 * 2**20),
        name="spread",
    )(row, own, *received)


def grad_kernel(flips, member_ref, stack, weights, *outs):
    for out, flip in zip(outs, flips):
        columns = pl.ds(pl.multiple_of((member_ref[0] ^ flip) * 512, 512), 512)
        out[...] = nn(stack[...], weights[:, columns]).astype(BF16)


def grads_for(flips, member, stack, weights):
    return pl.pallas_call(
        functools.partial(grad_kernel, flips),
        out_shape=[jax.ShapeDtypeStruct((PIXELS, 512), BF16)] * len(flips),
        in_specs=[pl.BlockSpec(memory_space=pltpu.SMEM)]
        + [pl.BlockSpec(memory_space=pltpu.VMEM)] * 2,
        out_specs=[pl.BlockSpec(memory_space=pltpu.VMEM)] * len(flips),
        compiler_params=pltpu.CompilerParams(vmem_limit_bytes=18 * 2**20),
        cost_estimate=pl.CostEstimate(
            flops=2 * PIXELS * 28 * W * 512 * len(flips), bytes_accessed=10**6, transcendentals=0
        ),
        name="grads_for",
    )(member, stack, weights)


def last_kernel(a, b, c, order_t, out):
    total = a[...].astype(F32) + b[...].astype(F32) + c[...].astype(F32)

    def put(at, value):
        out[at : at + 192, :] = value

    from_blocks(order_t[...], total.astype(BF16), put)


def last_sum(a, b, c, order_t):
    return pl.pallas_call(
        last_kernel,
        out_shape=jax.ShapeDtypeStruct((PIXELS, 512), BF16),
        in_specs=[pl.BlockSpec(memory_space=pltpu.VMEM)] * 4,
        out_specs=pl.BlockSpec(memory_space=pltpu.VMEM),
        compiler_params=pltpu.CompilerParams(vmem_limit_bytes=10 * 2**20),
        name="last_sum",
    )(a, b, c, order_t)


def flipped(x, bit):
    return lax.ppermute(x, "filt", [(i, i ^ bit) for i in range(lax.axis_size("filt"))])


def swapped(x, bits):
    pairs = [(r, r ^ bits) for r in range(8) if abs((r ^ bits) - r) <= 3]
    return lax.ppermute(x, "rows", pairs)


def on_device(
    features, point_weight, dilated_weight, branch_bias, project_weight, project_bias, cotangent
):
    row = lax.axis_index("rows").astype(jnp.int32).reshape(1)
    member = lax.axis_index("filt").astype(jnp.int32).reshape(1)
    order = jnp.asarray(order_matrix(), BF16)
    order_t = jnp.asarray(order_matrix().T, BF16)
    flat = features.reshape(PIXELS, CHANNELS)
    dilated = jnp.transpose(dilated_weight, (0, 1, 2, 4, 3)).reshape(27, W, CHANNELS)
    point = point_weight.T
    bias = branch_bias.reshape(1, 4 * W)
    flat, dilated, point = (
        pltpu.with_memory_space_constraint(x, pltpu.HBM) for x in (flat, dilated, point)
    )
    *sums, ordered, weights = odd_sums(row, flat, dilated, point, order)
    received = [swapped(sums[n], SWAPS[n]) for n in range(4)]
    sums = even_sums(row, ordered, weights)
    received += [swapped(sums[n], SWAPS[4 + n]) for n in range(2)]
    own = own_sums(ordered, weights, bias)
    acts = activations_of(row, own, received)
    across = flipped(acts, 2)
    beside = flipped(acts, 1)
    corner = flipped(across, 1)
    head_output, grads, *sends = head(
        row,
        member,
        (acts, beside, across, corner),
        project_weight,
        project_bias.reshape(1, 256),
        cotangent.reshape(PIXELS, 256),
        order,
        order_t,
    )
    arrived = [swapped(sends[n], x) for n, x in enumerate(SWAPS)]
    stack = spread(row, grads, arrived)
    near, far = grads_for((1, 3), member, stack, weights)
    near, far = flipped(near, 1), flipped(far, 1)
    (kept,) = grads_for((2,), member, stack, weights)
    crossing = (far.astype(F32) + kept.astype(F32)).astype(BF16)
    crossed = flipped(crossing, 2)
    later, crossing = lax.optimization_barrier((member, crossing))
    (kept,) = grads_for((0,), later, stack, weights)
    feature_grad = last_sum(kept, near, crossed, order_t)
    return head_output.reshape(12, 48, W), feature_grad.reshape(12, 48, 512)


def solution(mesh):
    body = on_device if fits(mesh) else on_device_general
    in_specs = (
        P("rows", None, None),
        P(None, "filt"),
        P(None, None, None, None, "filt"),
        P(None, "filt"),
        P(),
        P(),
        P("rows", None, None),
    )
    out_specs = (P("rows", None, "filt"), P("rows", None, "filt"))
    return jax.shard_map(
        body, mesh=mesh, in_specs=in_specs, out_specs=out_specs, check_vma=False
    )
```

profile of v0, /device:TPU:2, one launch (start us, length us, event | category | flops | bytes accessed | tf_op | source)
XLA Modules:
  0.0 93.0 jit_solution(7659861437033946188)
XLA Ops:
  0.6 0.9 copy-done.3
  1.5 8.7 %odd_sums.1 = (f32[288,128]{1,0:T(8,128)}, f32[288,128]{1,0:T(8,128)}, f32[288,128]{1,0:T(8,128)}, f32[288,128]{1,0:T(8,128)}, bf16[576,2048]{1,0:T(8,128)(2,1)S(1)}, /*index=5*/bf16[1792,2048]{1,0:T(8,128)(2,1)S(1)}) custom-call(s32[1]{0:T(128)} %bitcast.row_ref, bf16[576,2048]{1,0:T(8,128)(2,1)} %bitcast.14, bf16[27,64,2048]{2,1,0:T(8,128)(2,1)} %bitcast.13, ...), custom_call_target="tpu_custom_call" | custom-call | tf_op jit(solution)/shard_map/odd_sums/pallas_call | solution.py:266
  10.3 2.9 %even_sums.1 = (f32[288,128]{1,0:T(8,128)S(1)}, f32[288,128]{1,0:T(8,128)}) custom-call(s32[1]{0:T(128)} %bitcast.row_ref, bf16[576,2048]{1,0:T(8,128)(2,1)S(1)} %get-tuple-element.21.ordered, bf16[1792,2048]{1,0:T(8,128)(2,1)S(1)} %get-tuple-element.22.weights), custom_call_target="tpu_custom_call" | custom-call | flops 1000000 | bytes 10000 | tf_op jit(solution)/shard_map/even_sums/pallas_call | solution.py:300
  13.2 0.7 collective-permute-start.4
  13.9 4.5 %collective-permute-start.5 = (f32[288,128]{1,0:T(8,128)}, f32[288,128]{1,0:T(8,128)}, u32[]{:S(2)}, u32[]{:S(2)}) collective-permute-start(f32[288,128]{1,0:T(8,128)} %get-tuple-element.28), channel_id=1, source_target_pairs={{0,8},{4,12},{8,0},{12,4},{16,24},{20,28},{24,16},{28,20},{1,9},{5... | collective-permute-start | bytes 442376 | tf_op jit(solution)/shard_map/ppermute | solution.py:547
  18.4 1.9 %collective-permute-start = (f32[288,128]{1,0:T(8,128)}, f32[288,128]{1,0:T(8,128)}, u32[]{:S(2)}, u32[]{:S(2)}) collective-permute-start(f32[288,128]{1,0:T(8,128)} %get-tuple-element.23), channel_id=1, source_target_pairs={{4,16},{12,24},{16,4},{24,12},{5,17},{13,25},{17,5},{25,13},{6,18}... | collective-permute-start | bytes 442376 | tf_op jit(solution)/shard_map/ppermute | solution.py:547
  20.3 1.3 %collective-permute-start.1 = (f32[288,128]{1,0:T(8,128)}, f32[288,128]{1,0:T(8,128)}, u32[]{:S(2)}, u32[]{:S(2)}) collective-permute-start(f32[288,128]{1,0:T(8,128)} %get-tuple-element.24), channel_id=1, source_target_pairs={{8,20},{12,16},{16,12},{20,8},{9,21},{13,17},{17,13},{21,9},{10,22... | collective-permute-start | bytes 442376 | tf_op jit(solution)/shard_map/ppermute | solution.py:547
  21.6 1.4 %collective-permute-start.2 = (f32[288,128]{1,0:T(8,128)}, f32[288,128]{1,0:T(8,128)}, u32[]{:S(2)}, u32[]{:S(2)}) collective-permute-start(f32[288,128]{1,0:T(8,128)} %get-tuple-element.25), channel_id=1, source_target_pairs={{0,12},{4,8},{8,4},{12,0},{16,28},{20,24},{24,20},{28,16},{1,13},{... | collective-permute-start | bytes 442376 | tf_op jit(solution)/shard_map/ppermute | solution.py:547
  23.0 5.1 %collective-permute-start.3 = (f32[288,128]{1,0:T(8,128)}, f32[288,128]{1,0:T(8,128)}, u32[]{:S(2)}, u32[]{:S(2)}) collective-permute-start(f32[288,128]{1,0:T(8,128)} %get-tuple-element.26), channel_id=1, source_target_pairs={{0,4},{4,0},{8,12},{12,8},{16,20},{20,16},{24,28},{28,24},{1,5},{5... | collective-permute-start | bytes 442376 | tf_op jit(solution)/shard_map/ppermute | solution.py:547
  28.2 3.1 %copy-done.1 = bf16[1792,2048]{1,0:T(8,128)(2,1)S(1)} copy-done((bf16[1792,2048]{1,0:T(8,128)(2,1)S(1)}, bf16[1792,2048]{1,0:T(8,128)(2,1)}, u32[]{:S(2)}) %copy-start.1) | copy-done | bytes 7340056
  31.3 1.7 %own_sums.1.own = f32[576,256]{1,0:T(8,128)S(1)} custom-call(bf16[576,2048]{1,0:T(8,128)(2,1)S(1)} %get-tuple-element.21.ordered, bf16[1792,2048]{1,0:T(8,128)(2,1)S(1)} %copy-done.1, f32[1,256]{1,0:T(1,128)S(1)} %reshape.35.bias), custom_call_target="tpu_custom_call" | custom-call | flops 1000000 | bytes 10000 | tf_op jit(solution)/shard_map/own_sums/pallas_call | solution.py:339
  33.1 1.1 %collective-permute-done.3.refs_3_ = f32[288,128]{1,0:T(8,128)} collective-permute-done((f32[288,128]{1,0:T(8,128)}, f32[288,128]{1,0:T(8,128)}, u32[]{:S(2)}, u32[]{:S(2)}) %collective-permute-start.3) | collective-permute-done | bytes 147488 | tf_op jit(solution)/shard_map/ppermute | solution.py:547
  34.1 1.4 %activations.1.a0 = bf16[576,256]{1,0:T(8,128)(2,1)S(1)} custom-call(s32[1]{0:T(128)} %bitcast.row_ref, f32[576,256]{1,0:T(8,128)S(1)} %own_sums.1.own, f32[288,128]{1,0:T(8,128)} %collective-permute-done.refs_0_, f32[288,128]{1,0:T(8,128)} %collective-permute-done.1.refs_1_, f32[288,128]{1,0:T(8,128)} %collective-permute-done.2.refs_2_, ...), custom_call_target="tpu_custom_call" | custom-call | tf_op jit(solution)/shard_map/activations/pallas_call | solution.py:378
  35.6 1.6 %collective-permute-start.7 = (bf16[576,256]{1,0:T(8,128)(2,1)S(1)}, bf16[576,256]{1,0:T(8,128)(2,1)S(1)}, u32[]{:S(2)}, u32[]{:S(2)}) collective-permute-start(bf16[576,256]{1,0:T(8,128)(2,1)S(1)} %activations.1.a0), channel_id=1, source_target_pairs={{0,2},{1,3},{2,0},{3,1},{4,6},{5,7},{6,4},{7,5},{8,10},{9,11},{10,... | collective-permute-start | bytes 884744 | tf_op jit(solution)/shard_map/ppermute | solution.py:542
  37.2 7.4 %collective-permute-done.7.a2 = bf16[576,256]{1,0:T(8,128)(2,1)S(1)} collective-permute-done((bf16[576,256]{1,0:T(8,128)(2,1)S(1)}, bf16[576,256]{1,0:T(8,128)(2,1)S(1)}, u32[]{:S(2)}, u32[]{:S(2)}) %collective-permute-start.7) | collective-permute-done | bytes 294944 | tf_op jit(solution)/shard_map/ppermute | solution.py:542
  44.6 1.6 %collective-permute-done.8.a3 = bf16[576,256]{1,0:T(8,128)(2,1)S(1)} collective-permute-done((bf16[576,256]{1,0:T(8,128)(2,1)S(1)}, bf16[576,256]{1,0:T(8,128)(2,1)S(1)}, u32[]{:S(2)}, u32[]{:S(2)}) %collective-permute-start.8) | collective-permute-done | bytes 294944 | tf_op jit(solution)/shard_map/ppermute | solution.py:542
  46.2 2.0 %head.1 = (bf16[576,64]{1,0:T(8,128)(2,1)}, bf16[576,256]{1,0:T(8,128)(2,1)S(1)}, bf16[288,128]{1,0:T(8,128)(2,1)S(1)}, bf16[288,128]{1,0:T(8,128)(2,1)S(1)}, bf...) custom-call(s32[1]{0:T(128)} %bitcast.row_ref, ...), custom_call_target="tpu_custom_call" | custom-call | tf_op jit(solution)/shard_map/head/pallas_call | solution.py:431
  48.2 0.7 collective-permute-start.10
  48.9 4.9 %collective-permute-start.11 = (bf16[288,128]{1,0:T(8,128)(2,1)S(1)}, bf16[288,128]{1,0:T(8,128)(2,1)S(1)}, u32[]{:S(2)}, u32[]{:S(2)}) collective-permute-start(bf16[288,128]{1,0:T(8,128)(2,1)S(1)} %get-tuple-element.33), channel_id=1, source_target_pairs={{0,12},{4,8},{8,4},{12,0},{16,28},{20,24},{24,20},{28,16},{1,13},{... | collective-permute-start | bytes 221192 | tf_op jit(solution)/shard_map/ppermute | solution.py:547
  53.8 2.5 %collective-permute-start.12 = (bf16[288,128]{1,0:T(8,128)(2,1)S(1)}, bf16[288,128]{1,0:T(8,128)(2,1)S(1)}, u32[]{:S(2)}, u32[]{:S(2)}) collective-permute-start(bf16[288,128]{1,0:T(8,128)(2,1)S(1)} %get-tuple-element.34), channel_id=1, source_target_pairs={{0,4},{4,0},{8,12},{12,8},{16,20},{20,16},{24,28},{28,24},{1,5},{5... | collective-permute-start | bytes 221192 | tf_op jit(solution)/shard_map/ppermute | solution.py:547
  56.3 0.7 collective-permute-start.13
  57.0 2.4 %collective-permute-start.14 = (bf16[288,128]{1,0:T(8,128)(2,1)S(1)}, bf16[288,128]{1,0:T(8,128)(2,1)S(1)}, u32[]{:S(2)}, u32[]{:S(2)}) collective-permute-start(bf16[288,128]{1,0:T(8,128)(2,1)S(1)} %get-tuple-element.36), channel_id=1, source_target_pairs={{0,8},{4,12},{8,0},{12,4},{16,24},{20,28},{24,16},{28,20},{1,9},{5... | collective-permute-start | bytes 221192 | tf_op jit(solution)/shard_map/ppermute | solution.py:547
  59.4 2.9 %collective-permute-start.9 = (bf16[288,128]{1,0:T(8,128)(2,1)S(1)}, bf16[288,128]{1,0:T(8,128)(2,1)S(1)}, u32[]{:S(2)}, u32[]{:S(2)}) collective-permute-start(bf16[288,128]{1,0:T(8,128)(2,1)S(1)} %get-tuple-element.31), channel_id=1, source_target_pairs={{4,16},{12,24},{16,4},{24,12},{5,17},{13,25},{17,5},{25,13},{6,18}... | collective-permute-start | bytes 221192 | tf_op jit(solution)/shard_map/ppermute | solution.py:547
  62.3 5.7 %collective-permute-done.9.refs_0_ = bf16[288,128]{1,0:T(8,128)(2,1)S(1)} collective-permute-done((bf16[288,128]{1,0:T(8,128)(2,1)S(1)}, bf16[288,128]{1,0:T(8,128)(2,1)S(1)}, u32[]{:S(2)}, u32[]{:S(2)}) %collective-permute-start.9) | collective-permute-done | bytes 73760 | tf_op jit(solution)/shard_map/ppermute | solution.py:547
  68.1 0.6 spread.1.stack
  68.7 3.1 %copy-done.2 = bf16[1792,2048]{1,0:T(8,128)(2,1)S(1)} copy-done((bf16[1792,2048]{1,0:T(8,128)(2,1)S(1)}, bf16[1792,2048]{1,0:T(8,128)(2,1)}, u32[]{:S(2)}) %copy-start.2) | copy-done | bytes 7340056
  71.7 2.3 %grads_for.3 = (bf16[576,512]{1,0:T(8,128)(2,1)S(1)}, bf16[576,512]{1,0:T(8,128)(2,1)S(1)}) custom-call(s32[1]{0:T(128)} %bitcast.1.member_ref, bf16[576,1792]{1,0:T(8,128)(2,1)S(1)} %spread.1.stack, bf16[1792,2048]{1,0:T(8,128)(2,1)S(1)} %copy-done.2), custom_call_target="tpu_custom_call" | custom-call | flops 2113929216 | bytes 1000000 | tf_op jit(solution)/shard_map/grads_for/pallas_call | solution.py:507
  74.6 1.2 %grads_for.4 = bf16[576,512]{1,0:T(8,128)(2,1)S(1)} custom-call(s32[1]{0:T(128)} %bitcast.1.member_ref, bf16[576,1792]{1,0:T(8,128)(2,1)S(1)} %spread.1.stack, bf16[1792,2048]{1,0:T(8,128)(2,1)S(1)} %copy-done.2), custom_call_target="tpu_custom_call" | custom-call | flops 1056964608 | bytes 1000000 | tf_op jit(solution)/shard_map/grads_for/pallas_call | solution.py:507
  76.3 1.6 %collective-permute-start.17 = (bf16[576,512]{1,0:T(8,128)(2,1)S(1)}, bf16[576,512]{1,0:T(8,128)(2,1)S(1)}, u32[]{:S(2)}, u32[]{:S(2)}) collective-permute-start(bf16[576,512]{1,0:T(8,128)(2,1)S(1)} %add_convert_fusion), channel_id=1, source_target_pairs={{0,2},{1,3},{2,0},{3,1},{4,6},{5,7},{6,4},{7,5},{8,10},{9,11},{10,... | collective-permute-start | bytes 1769480 | tf_op jit(solution)/shard_map/ppermute | solution.py:542
  77.9 1.2 %grads_for.5.a = bf16[576,512]{1,0:T(8,128)(2,1)S(1)} custom-call(s32[1]{0:T(128)} %bitcast.1.member_ref, bf16[576,1792]{1,0:T(8,128)(2,1)S(1)} %spread.1.stack, bf16[1792,2048]{1,0:T(8,128)(2,1)S(1)} %copy-done.2), custom_call_target="tpu_custom_call" | custom-call | flops 1056964608 | bytes 1000000 | tf_op jit(solution)/shard_map/grads_for/pallas_call | solution.py:507
  79.1 12.6 %collective-permute-done.17.c = bf16[576,512]{1,0:T(8,128)(2,1)S(1)} collective-permute-done((bf16[576,512]{1,0:T(8,128)(2,1)S(1)}, bf16[576,512]{1,0:T(8,128)(2,1)S(1)}, u32[]{:S(2)}, u32[]{:S(2)}) %collective-permute-start.17) | collective-permute-done | bytes 589856 | tf_op jit(solution)/shard_map/ppermute | solution.py:542
  91.7 1.3 %last_sum.1 = bf16[576,512]{1,0:T(8,128)(2,1)} custom-call(bf16[576,512]{1,0:T(8,128)(2,1)S(1)} %grads_for.5.a, bf16[576,512]{1,0:T(8,128)(2,1)S(1)} %collective-permute-done.16.b, bf16[576,512]{1,0:T(8,128)(2,1)S(1)} %collective-permute-done.17.c, bf16[192,192]{1,0:T(8,128)(2,1)S(1)} %copy-done.4), custom_call_target="tpu_custom_call" | custom-call | tf_op jit(solution)/shard_map/last_sum/pallas_call | solution.py:531
  (34 shorter events, 1.2 us)
Async XLA Ops:
  0.6 0.9 copy-start.3
  10.2 3.0 %copy-start = (bf16[1792,2048]{1,0:T(8,128)(2,1)}, bf16[1792,2048]{1,0:T(8,128)(2,1)S(1)}, u32[]{:S(2)}) copy-start(bf16[1792,2048]{1,0:T(8,128)(2,1)S(1)} %get-tuple-element.22.weights) | copy-start | bytes 22020100
  10.3 17.8 %copy-start.8 = (f32[4,64]{1,0:T(4,128)S(1)}, f32[4,64]{1,0:T(4,128)}, u32[]{:S(2)}) copy-start(f32[4,64]{1,0:T(4,128)} %param.12) | copy-start | bytes 3076
  13.2 9.8 %collective-permute-start.4 = (f32[288,128]{1,0:T(8,128)S(1)}, f32[288,128]{1,0:T(8,128)S(1)}, u32[]{:S(2)}, u32[]{:S(2)}) collective-permute-start(f32[288,128]{1,0:T(8,128)S(1)} %get-tuple-element.27), channel_id=1, source_target_pairs={{8,16},{12,20},{16,8},{20,12},{9,17},{13,21},{17,9},{21,13},{10,18... | collective-permute-start | bytes 442376 | tf_op jit(solution)/shard_map/ppermute | solution.py:547
  13.9 19.1 %collective-permute-start.5 = (f32[288,128]{1,0:T(8,128)}, f32[288,128]{1,0:T(8,128)}, u32[]{:S(2)}, u32[]{:S(2)}) collective-permute-start(f32[288,128]{1,0:T(8,128)} %get-tuple-element.28), channel_id=1, source_target_pairs={{0,8},{4,12},{8,0},{12,4},{16,24},{20,28},{24,16},{28,20},{1,9},{5... | collective-permute-start | bytes 442376 | tf_op jit(solution)/shard_map/ppermute | solution.py:547
  18.4 14.7 %collective-permute-start = (f32[288,128]{1,0:T(8,128)}, f32[288,128]{1,0:T(8,128)}, u32[]{:S(2)}, u32[]{:S(2)}) collective-permute-start(f32[288,128]{1,0:T(8,128)} %get-tuple-element.23), channel_id=1, source_target_pairs={{4,16},{12,24},{16,4},{24,12},{5,17},{13,25},{17,5},{25,13},{6,18}... | collective-permute-start | bytes 442376 | tf_op jit(solution)/shard_map/ppermute | solution.py:547
  20.3 12.8 %collective-permute-start.1 = (f32[288,128]{1,0:T(8,128)}, f32[288,128]{1,0:T(8,128)}, u32[]{:S(2)}, u32[]{:S(2)}) collective-permute-start(f32[288,128]{1,0:T(8,128)} %get-tuple-element.24), channel_id=1, source_target_pairs={{8,20},{12,16},{16,12},{20,8},{9,21},{13,17},{17,13},{21,9},{10,22... | collective-permute-start | bytes 442376 | tf_op jit(solution)/shard_map/ppermute | solution.py:547
  21.6 11.4 %collective-permute-start.2 = (f32[288,128]{1,0:T(8,128)}, f32[288,128]{1,0:T(8,128)}, u32[]{:S(2)}, u32[]{:S(2)}) collective-permute-start(f32[288,128]{1,0:T(8,128)} %get-tuple-element.25), channel_id=1, source_target_pairs={{0,12},{4,8},{8,4},{12,0},{16,28},{20,24},{24,20},{28,16},{1,13},{... | collective-permute-start | bytes 442376 | tf_op jit(solution)/shard_map/ppermute | solution.py:547
  23.0 11.1 %collective-permute-start.3 = (f32[288,128]{1,0:T(8,128)}, f32[288,128]{1,0:T(8,128)}, u32[]{:S(2)}, u32[]{:S(2)}) collective-permute-start(f32[288,128]{1,0:T(8,128)} %get-tuple-element.26), channel_id=1, source_target_pairs={{0,4},{4,0},{8,12},{12,8},{16,20},{20,16},{24,28},{28,24},{1,5},{5... | collective-permute-start | bytes 442376 | tf_op jit(solution)/shard_map/ppermute | solution.py:547
  28.2 3.1 %copy-start.1 = (bf16[1792,2048]{1,0:T(8,128)(2,1)S(1)}, bf16[1792,2048]{1,0:T(8,128)(2,1)}, u32[]{:S(2)}) copy-start(bf16[1792,2048]{1,0:T(8,128)(2,1)} %copy-done) | copy-start | bytes 22020100
  31.3 14.9 %copy-start.4 = (bf16[192,192]{1,0:T(8,128)(2,1)S(1)}, bf16[192,192]{1,0:T(8,128)(2,1)}, u32[]{:S(2)}) copy-start(bf16[192,192]{1,0:T(8,128)(2,1)} %constant.11.clone.order.order_t) | copy-start | bytes 221188
  31.3 14.9 %copy-start.5 = (bf16[4,256,256]{2,1,0:T(8,128)(2,1)S(1)}, bf16[4,256,256]{2,1,0:T(8,128)(2,1)}, u32[]{:S(2)}) copy-start(bf16[4,256,256]{2,1,0:T(8,128)(2,1)} %project.1) | copy-start | bytes 1572868
  31.3 14.9 %copy-start.6 = (bf16[12,48,256]{2,1,0:T(8,128)(2,1)S(1)}, bf16[12,48,256]{2,1,0:T(8,128)(2,1)}, u32[]{:S(2)}) copy-start(bf16[12,48,256]{2,1,0:T(8,128)(2,1)} %param.15) | copy-start | bytes 884740
  31.3 14.9 %copy-start.7 = (f32[256]{0:T(256)S(1)}, f32[256]{0:T(256)}, u32[]{:S(2)}) copy-start(f32[256]{0:T(256)} %param.14) | copy-start | bytes 3076
  35.6 9.0 %collective-permute-start.7 = (bf16[576,256]{1,0:T(8,128)(2,1)S(1)}, bf16[576,256]{1,0:T(8,128)(2,1)S(1)}, u32[]{:S(2)}, u32[]{:S(2)}) collective-permute-start(bf16[576,256]{1,0:T(8,128)(2,1)S(1)} %activations.1.a0), channel_id=1, source_target_pairs={{0,2},{1,3},{2,0},{3,1},{4,6},{5,7},{6,4},{7,5},{8,10},{9,11},{10,... | collective-permute-start | bytes 884744 | tf_op jit(solution)/shard_map/ppermute | solution.py:542
  37.2 7.4 %collective-permute-start.6 = (bf16[576,256]{1,0:T(8,128)(2,1)S(1)}, bf16[576,256]{1,0:T(8,128)(2,1)S(1)}, u32[]{:S(2)}, u32[]{:S(2)}) collective-permute-start(bf16[576,256]{1,0:T(8,128)(2,1)S(1)} %activations.1.a0), channel_id=1, source_target_pairs={{0,1},{1,0},{2,3},{3,2},{4,5},{5,4},{6,7},{7,6},{8,9},{9,8},{10,11... | collective-permute-start | bytes 884744 | tf_op jit(solution)/shard_map/ppermute | solution.py:542
  44.6 1.6 %collective-permute-start.8 = (bf16[576,256]{1,0:T(8,128)(2,1)S(1)}, bf16[576,256]{1,0:T(8,128)(2,1)S(1)}, u32[]{:S(2)}, u32[]{:S(2)}) collective-permute-start(bf16[576,256]{1,0:T(8,128)(2,1)S(1)} %collective-permute-done.7.a2), channel_id=1, source_target_pairs={{0,1},{1,0},{2,3},{3,2},{4,5},{5,4},{6,7},{7,6},{8,9},{9,8},{10,11... | collective-permute-start | bytes 884744 | tf_op jit(solution)/shard_map/ppermute | solution.py:542
  48.2 11.1 %collective-permute-start.10 = (bf16[288,128]{1,0:T(8,128)(2,1)S(1)}, bf16[288,128]{1,0:T(8,128)(2,1)S(1)}, u32[]{:S(2)}, u32[]{:S(2)}) collective-permute-start(bf16[288,128]{1,0:T(8,128)(2,1)S(1)} %get-tuple-element.32), channel_id=1, source_target_pairs={{8,20},{12,16},{16,12},{20,8},{9,21},{13,17},{17,13},{21,9},{10,22... | collective-permute-start | bytes 221192 | tf_op jit(solution)/shard_map/ppermute | solution.py:547
  48.9 13.4 %collective-permute-start.11 = (bf16[288,128]{1,0:T(8,128)(2,1)S(1)}, bf16[288,128]{1,0:T(8,128)(2,1)S(1)}, u32[]{:S(2)}, u32[]{:S(2)}) collective-permute-start(bf16[288,128]{1,0:T(8,128)(2,1)S(1)} %get-tuple-element.33), channel_id=1, source_target_pairs={{0,12},{4,8},{8,4},{12,0},{16,28},{20,24},{24,20},{28,16},{1,13},{... | collective-permute-start | bytes 221192 | tf_op jit(solution)/shard_map/ppermute | solution.py:547
  53.8 8.5 %collective-permute-start.12 = (bf16[288,128]{1,0:T(8,128)(2,1)S(1)}, bf16[288,128]{1,0:T(8,128)(2,1)S(1)}, u32[]{:S(2)}, u32[]{:S(2)}) collective-permute-start(bf16[288,128]{1,0:T(8,128)(2,1)S(1)} %get-tuple-element.34), channel_id=1, source_target_pairs={{0,4},{4,0},{8,12},{12,8},{16,20},{20,16},{24,28},{28,24},{1,5},{5... | collective-permute-start | bytes 221192 | tf_op jit(solution)/shard_map/ppermute | solution.py:547
  56.3 6.0 %collective-permute-start.13 = (bf16[288,128]{1,0:T(8,128)(2,1)S(1)}, bf16[288,128]{1,0:T(8,128)(2,1)S(1)}, u32[]{:S(2)}, u32[]{:S(2)}) collective-permute-start(bf16[288,128]{1,0:T(8,128)(2,1)S(1)} %get-tuple-element.35), channel_id=1, source_target_pairs={{8,16},{12,20},{16,8},{20,12},{9,17},{13,21},{17,9},{21,13},{10,18... | collective-permute-start | bytes 221192 | tf_op jit(solution)/shard_map/ppermute | solution.py:547
  57.0 5.4 %collective-permute-start.14 = (bf16[288,128]{1,0:T(8,128)(2,1)S(1)}, bf16[288,128]{1,0:T(8,128)(2,1)S(1)}, u32[]{:S(2)}, u32[]{:S(2)}) collective-permute-start(bf16[288,128]{1,0:T(8,128)(2,1)S(1)} %get-tuple-element.36), channel_id=1, source_target_pairs={{0,8},{4,12},{8,0},{12,4},{16,24},{20,28},{24,16},{28,20},{1,9},{5... | collective-permute-start | bytes 221192 | tf_op jit(solution)/shard_map/ppermute | solution.py:547
  59.4 8.7 %collective-permute-start.9 = (bf16[288,128]{1,0:T(8,128)(2,1)S(1)}, bf16[288,128]{1,0:T(8,128)(2,1)S(1)}, u32[]{:S(2)}, u32[]{:S(2)}) collective-permute-start(bf16[288,128]{1,0:T(8,128)(2,1)S(1)} %get-tuple-element.31), channel_id=1, source_target_pairs={{4,16},{12,24},{16,4},{24,12},{5,17},{13,25},{17,5},{25,13},{6,18}... | collective-permute-start | bytes 221192 | tf_op jit(solution)/shard_map/ppermute | solution.py:547
  68.7 3.1 %copy-start.2 = (bf16[1792,2048]{1,0:T(8,128)(2,1)S(1)}, bf16[1792,2048]{1,0:T(8,128)(2,1)}, u32[]{:S(2)}) copy-start(bf16[1792,2048]{1,0:T(8,128)(2,1)} %copy-done) | copy-start | bytes 22020100
  74.0 2.1 %collective-permute-start.15 = (bf16[576,512]{1,0:T(8,128)(2,1)S(1)}, bf16[576,512]{1,0:T(8,128)(2,1)S(1)}, u32[]{:S(2)}, u32[]{:S(2)}) collective-permute-start(bf16[576,512]{1,0:T(8,128)(2,1)S(1)} %get-tuple-element.37), channel_id=1, source_target_pairs={{0,1},{1,0},{2,3},{3,2},{4,5},{5,4},{6,7},{7,6},{8,9},{9,8},{10,11... | collective-permute-start | bytes 1769480 | tf_op jit(solution)/shard_map/ppermute | solution.py:542
  74.1 5.0 %collective-permute-start.16 = (bf16[576,512]{1,0:T(8,128)(2,1)S(1)}, bf16[576,512]{1,0:T(8,128)(2,1)S(1)}, u32[]{:S(2)}, u32[]{:S(2)}) collective-permute-start(bf16[576,512]{1,0:T(8,128)(2,1)S(1)} %get-tuple-element.39), channel_id=1, source_target_pairs={{0,1},{1,0},{2,3},{3,2},{4,5},{5,4},{6,7},{7,6},{8,9},{9,8},{10,11... | collective-permute-start | bytes 1769480 | tf_op jit(solution)/shard_map/ppermute | solution.py:542
  76.3 15.4 %collective-permute-start.17 = (bf16[576,512]{1,0:T(8,128)(2,1)S(1)}, bf16[576,512]{1,0:T(8,128)(2,1)S(1)}, u32[]{:S(2)}, u32[]{:S(2)}) collective-permute-start(bf16[576,512]{1,0:T(8,128)(2,1)S(1)} %add_convert_fusion), channel_id=1, source_target_pairs={{0,2},{1,3},{2,0},{3,1},{4,6},{5,7},{6,4},{7,5},{8,10},{9,11},{10,... | collective-permute-start | bytes 1769480 | tf_op jit(solution)/shard_map/ppermute | solution.py:542
where the time goes:
time: 93.3 us; the launch traced here: 93 us
  starting transfers between devices  32.6 us (35%)
  waiting for transfers between devices  28.7 us (31%)
  Pallas kernels  23.4 us (25%)
  local copies, waits for them, and re-layouts  7.26 us (8%)
    ppermute x12, starting transfers between devices, swapped(): return lax.ppermute(x, 'rows', pairs)  28.9 us
    ppermute x6, waiting for transfers between devices, flipped(): lax.ppermute(x, 'filt', [(i, i ^ bit) for i in range(lax.axis_size('filt'...  21.8 us
    pallas_call x1, Pallas kernels, odd_sums(): pl.pallas_call(odd_kernel, out_shape=[jax.ShapeDtypeStruct((HALF, 128), F...  8.7 us
    unnamed x18, local copies, waits for them, and re-layouts  7.18 us
    ppermute x12, waiting for transfers between devices, swapped(): return lax.ppermute(x, 'rows', pairs)  6.84 us
    pallas_call x3, Pallas kernels, grads_for(): pl.pallas_call(functools.partial(grad_kernel, flips), out_shape=[jax.Shap...  4.76 us
    ppermute x6, starting transfers between devices, flipped(): lax.ppermute(x, 'filt', [(i, i ^ bit) for i in range(lax.axis_size('filt'...  3.74 us
    pallas_call x1, Pallas kernels, even_sums(): pl.pallas_call(even_kernel, out_shape=[jax.ShapeDtypeStruct((HALF, 128),...  2.85 us
  transfers between devices with their start and end apart: 18, of which 6 were waited for; matrix products, arithmetic and copies ran while one was open for 0% of the time, Pallas kernels for 5%

commit v1 on v0

--- a/solution.py
+++ b/solution.py
@@ -2,7 +2,6 @@
 
 import jax
 import jax.numpy as jnp
-import numpy as np
 from jax import lax
 from jax.experimental import pallas as pl
 from jax.experimental.pallas import tpu as pltpu
@@ -154,19 +153,25 @@
 )
 ODD_AT, EVEN_AT, LEFT_AT, RIGHT_AT = 4 * W, 16 * W, 22 * W, 25 * W
 SWAPS = (5, 7, 3, 1, 6, 2)
+GRAD_SWAPS = (1, 5, 7, 3, 6, 2)
 
 
 def fits(mesh):
     return mesh.shape["rows"] == 8 and mesh.shape["filt"] == 4
 
 
-def order_matrix():
-    to = np.zeros((192, 192), np.float32)
-    for m in range(4):
-        for r in range(4):
-            for c in range(12):
-                to[m * 48 + r * 12 + c, r * 48 + m * 12 + c] = 1
-    return to
+def order_matrix(turned=False):
+    to = lax.broadcasted_iota(jnp.int32, (192, 192), 1 if turned else 0)
+    source = lax.broadcasted_iota(jnp.int32, (192, 192), 0 if turned else 1)
+
+    def parts(value, width):
+        return sum((value >= n * width).astype(jnp.int32) for n in (1, 2, 3))
+
+    block = parts(to, 48)
+    within = to - 48 * block
+    line = parts(within, 12)
+    wanted = line * 48 + block * 12 + within - 12 * line
+    return (source == wanted).astype(F32).astype(BF16)
 
 
 def tap_index(tap):
@@ -180,13 +185,6 @@
 
 def nn(a, b):
     return lax.dot_general(a, b, (((1,), (0,)), ((), ())), preferred_element_type=F32)
-
-
-def into_blocks(order, read, write):
-    for g in range(3):
-        moved = nn(order, read(g * 192)).astype(BF16)
-        for m in range(4):
-            write(m * BLOCK + g * 48, moved[m * 48 : (m + 1) * 48])
 
 
 def from_blocks(order_t, value, write):
@@ -213,7 +211,8 @@
     packed[k + 2] = jnp.where(low, pltpu.roll(top, W, 1), bottom)
 
 
-def odd_kernel(row_ref, features, dilated, point, order, *refs):
+def odd_kernel(features, dilated, point, *refs):
+    row = lax.axis_index("rows")
     out, ordered, weights = refs[0:4], refs[4], refs[5]
     raw, sums, packed, feature_sems, weight_sems = refs[6:]
     loads = []
@@ -230,11 +229,18 @@
                 weight_sems.at[q + 1],
             )
         )
-    for fetch in fetches[4:] + fetches[:4]:
-        fetch.start()
+    queue = fetches[4:] + fetches[:4]
+
+    def start_loads(first, last):
+        for fetch in queue[first:last]:
+            fetch.start()
+
+    start_loads(0, 4)
+    order = order_matrix()
     for g in range(3):
         loads[g].wait()
-        moved = nn(order[...], raw[g * 192 : (g + 1) * 192, :]).astype(BF16)
+        start_loads(4 + 4 * g, 8 + 4 * g)
+        moved = nn(order, raw[g * 192 : (g + 1) * 192, :]).astype(BF16)
         for m in range(4):
             at = m * BLOCK + g * 48
             ordered[at : at + 48, :] = moved[m * 48 : (m + 1) * 48]
@@ -246,9 +252,11 @@
         return nt(ordered[first * BLOCK : last * BLOCK, :], weights[at : at + 256, :])
 
     d = product(0, 0, 4)
+    start_loads(16, 22)
     sums[2] = d[:, :128]
     sums[0] = d[:, 128:]
     d = product(2, 0, 3)
+    start_loads(22, 28)
     sums[2, 3 * BLOCK :, :] = sums[2, 3 * BLOCK :, :] + d[:BLOCK, :128]
     sums[0, BLOCK:, :] = sums[0, BLOCK:, :] + d[:, 128:]
     d = product(4, 1, 4)
@@ -257,19 +265,17 @@
     pack_rows(sums, packed, 3)
     pack_rows(sums, packed, 1)
     for n in range(4):
-        out[n][...] = packed[outward_slot(row_ref[0], SWAPS[n])]
+        out[n][...] = packed[outward_slot(row, SWAPS[n])]
     for fetch in fetches[:4] + fetches[16:]:
         fetch.wait()
 
 
-def odd_sums(row, features, dilated, point, order):
+def odd_sums(features, dilated, point):
     return pl.pallas_call(
         odd_kernel,
         out_shape=[jax.ShapeDtypeStruct((HALF, 128), F32)] * 4
         + [pltpu.VMEM((PIXELS, CHANNELS), BF16), pltpu.VMEM((28 * W, CHANNELS), BF16)],
-        in_specs=[pl.BlockSpec(memory_space=pltpu.SMEM)]
-        + [pl.BlockSpec(memory_space=pltpu.HBM)] * 3
-        + [pl.BlockSpec(memory_space=pltpu.VMEM)],
+        in_specs=[pl.BlockSpec(memory_space=pltpu.HBM)] * 3,
         out_specs=[pl.BlockSpec(memory_space=pltpu.VMEM)] * 6,
         scratch_shapes=[
             pltpu.VMEM((PIXELS, CHANNELS), BF16),
@@ -280,30 +286,31 @@
         ],
         compiler_params=pltpu.CompilerParams(vmem_limit_bytes=28 * 2**20),
         name="odd_sums",
-    )(row, features, dilated, point, order)
-
-
-def even_kernel(row_ref, ordered, weights, *refs):
-    out = refs[0:2]
-    sums, packed = refs[2:]
+    )(features, dilated, point)
+
+
+def even_kernel(ordered, weights, *refs):
+    row = lax.axis_index("rows")
+    out = refs[1:3]
+    sums, packed = refs[3:]
     d = nt(ordered[...], weights[EVEN_AT : EVEN_AT + 384, :])
     sums[1] = d[:, :128]
     sums[1, 2 * BLOCK :, :] = sums[1, 2 * BLOCK :, :] + d[: 2 * BLOCK, 128:256]
     sums[1, : 2 * BLOCK, :] = sums[1, : 2 * BLOCK, :] + d[2 * BLOCK :, 256:]
     pack_rows(sums, packed, 2)
     for n in range(2):
-        slot = jnp.where((row_ref[0] ^ SWAPS[4 + n]) < row_ref[0], 4, 1)
+        slot = jnp.where((row ^ SWAPS[4 + n]) < row, 4, 1)
         out[n][...] = packed[slot]
 
 
-def even_sums(row, ordered, weights):
+def even_sums(ordered, weights, started):
     return pl.pallas_call(
         even_kernel,
         out_shape=[jax.ShapeDtypeStruct((HALF, 128), F32)] * 2,
         in_specs=[
-            pl.BlockSpec(memory_space=pltpu.SMEM),
             pl.BlockSpec(memory_space=pltpu.VMEM),
             pl.BlockSpec(memory_space=pltpu.VMEM),
+            pl.BlockSpec(memory_space=pl.ANY),
         ],
         out_specs=[pl.BlockSpec(memory_space=pltpu.VMEM)] * 2,
         scratch_shapes=[
@@ -313,11 +320,12 @@
         compiler_params=pltpu.CompilerParams(vmem_limit_bytes=18 * 2**20),
         cost_estimate=pl.CostEstimate(flops=10**6, bytes_accessed=10**4, transcendentals=0),
         name="even_sums",
-    )(row, ordered, weights)
+    )(ordered, weights, started)
 
 
 def own_kernel(ordered, weights, bias, out):
-    out[...] = nt(ordered[...], weights[:256, :]) + bias[...]
+    line = jnp.concatenate([bias[k : k + 1, :] for k in range(4)], 1)
+    out[...] = nt(ordered[...], weights[:256, :]) + line
     low = low_lanes((PIXELS, 128))
 
     def add(first, value, k):
@@ -351,16 +359,16 @@
     return jnp.where((other >= 0) & (other < 8), row ^ other, 0)
 
 
-def gather_arrivals(recv, arrivals):
+def gather_arrivals(recv, arrivals, swaps):
     arrivals[0] = jnp.zeros((HALF, 128), arrivals.dtype)
-    for n, x in enumerate(SWAPS):
+    for n, x in enumerate(swaps):
         arrivals[x] = recv[n][...]
 
 
-def activation_kernel(row_ref, own, *refs):
+def activation_kernel(own, *refs):
     recv, acts, arrivals = refs[:6], refs[6], refs[7]
-    row = row_ref[0]
-    gather_arrivals(recv, arrivals)
+    row = lax.axis_index("rows")
+    gather_arrivals(recv, arrivals, SWAPS)
     low = low_lanes((HALF, 128))
     t1, t2, t3 = (
         arrivals[arrival_slot(row, row - k)] + arrivals[arrival_slot(row, row + k)]
@@ -374,22 +382,21 @@
         acts[rows, 128:] = jnp.maximum(right, 0.0).astype(BF16)
 
 
-def activations_of(row, own, received):
+def activations_of(own, received):
     return pl.pallas_call(
         activation_kernel,
         out_shape=jax.ShapeDtypeStruct((PIXELS, 4 * W), BF16),
-        in_specs=[pl.BlockSpec(memory_space=pltpu.SMEM)]
-        + [pl.BlockSpec(memory_space=pltpu.VMEM)] * 7,
+        in_specs=[pl.BlockSpec(memory_space=pltpu.VMEM)] * 7,
         out_specs=pl.BlockSpec(memory_space=pltpu.VMEM),
         scratch_shapes=[pltpu.VMEM((8, HALF, 128), F32)],
         compiler_params=pltpu.CompilerParams(vmem_limit_bytes=8 * 2**20),
         name="activations",
-    )(row, own, *received)
-
-
-def head_kernel(row_ref, member_ref, a0, a1, a2, a3, project, bias, cotangent, order, order_t, *refs):
+    )(own, *received)
+
+
+def head_kernel(a0, a1, a2, a3, project, bias, cotangent, *refs):
     head_out, grads, sends, ordered, packed = refs[0], refs[1], refs[2:8], refs[8], refs[9]
-    member = member_ref[0]
+    row, member = lax.axis_index("rows"), lax.axis_index("filt")
 
     def rows_of(who):
         at = pl.multiple_of(who * W, W)
@@ -407,9 +414,10 @@
     def put(at, value):
         head_out[at : at + 192, :] = value
 
-    from_blocks(order_t[...], mine, put)
+    from_blocks(order_matrix(True), mine, put)
+    order = order_matrix()
     for g in range(3):
-        moved = nn(order[...], cotangent[g * 192 : (g + 1) * 192, :])
+        moved = nn(order, cotangent[g * 192 : (g + 1) * 192, :])
         for m in range(4):
             at = m * BLOCK + g * 48
             ordered[at : at + 48, :] = moved[m * 48 : (m + 1) * 48]
@@ -422,12 +430,12 @@
     packed[0] = jnp.where(low, pltpu.roll(left[:HALF], W, 1), left[HALF:]).astype(BF16)
     packed[1] = jnp.where(low, right[:HALF], pltpu.roll(right[HALF:], W, 1)).astype(BF16)
     packed[2] = jnp.where(low, pltpu.roll(right[:HALF], W, 1), right[HALF:]).astype(BF16)
-    for n, x in enumerate(SWAPS):
-        apart = jnp.abs((row_ref[0] ^ x) - row_ref[0])
+    for n, x in enumerate(GRAD_SWAPS):
+        apart = jnp.abs((row ^ x) - row)
         sends[n][...] = packed[jnp.where(apart <= 3, apart - 1, 0)]
 
 
-def head(row, member, acts, project, bias, cotangent, order, order_t):
+def head(acts, project, bias, cotangent):
     return pl.pallas_call(
         head_kernel,
         out_shape=[
@@ -435,19 +443,18 @@
             jax.ShapeDtypeStruct((PIXELS, 4 * W), BF16),
         ]
         + [jax.ShapeDtypeStruct((HALF, 128), BF16)] * 6,
-        in_specs=[pl.BlockSpec(memory_space=pltpu.SMEM)] * 2
-        + [pl.BlockSpec(memory_space=pltpu.VMEM)] * 9,
+        in_specs=[pl.BlockSpec(memory_space=pltpu.VMEM)] * 7,
         out_specs=[pl.BlockSpec(memory_space=pltpu.VMEM)] * 8,
         scratch_shapes=[pltpu.VMEM((PIXELS, 256), F32), pltpu.VMEM((3, HALF, 128), BF16)],
         compiler_params=pltpu.CompilerParams(vmem_limit_bytes=12 * 2**20),
         name="head",
-    )(row, member, *acts, project, bias, cotangent, order, order_t)
-
-
-def spread_kernel(row_ref, own, *refs):
+    )(*acts, project, bias, cotangent)
+
+
+def spread_kernel(own, *refs):
     recv, stack, arrivals, pairs, twice = refs[:6], refs[6], refs[7], refs[8], refs[9]
-    row = row_ref[0]
-    gather_arrivals(recv, arrivals)
+    row = lax.axis_index("rows")
+    gather_arrivals(recv, arrivals, GRAD_SWAPS)
     low = low_lanes((HALF, 128))
     low_all = low_lanes((PIXELS, 128))
     for k in (1, 2, 3):
@@ -480,12 +487,11 @@
             )
 
 
-def spread(row, own, received):
+def spread(own, received):
     return pl.pallas_call(
         spread_kernel,
         out_shape=pltpu.VMEM((PIXELS, 28 * W), BF16),
-        in_specs=[pl.BlockSpec(memory_space=pltpu.SMEM)]
-        + [pl.BlockSpec(memory_space=pltpu.VMEM)] * 7,
+        in_specs=[pl.BlockSpec(memory_space=pltpu.VMEM)] * 7,
         out_specs=pl.BlockSpec(memory_space=pltpu.VMEM),
         scratch_shapes=[
             pltpu.VMEM((8, HALF, 128), BF16),
@@ -494,48 +500,48 @@
         ],
         compiler_params=pltpu.CompilerParams(vmem_limit_bytes=12 * 2**20),
         name="spread",
-    )(row, own, *received)
-
-
-def grad_kernel(flips, member_ref, stack, weights, *outs):
+    )(own, *received)
+
+
+def grad_kernel(flips, stack, weights, *outs):
+    member = lax.axis_index("filt")
     for out, flip in zip(outs, flips):
-        columns = pl.ds(pl.multiple_of((member_ref[0] ^ flip) * 512, 512), 512)
+        columns = pl.ds(pl.multiple_of((member ^ flip) * 512, 512), 512)
         out[...] = nn(stack[...], weights[:, columns]).astype(BF16)
 
 
-def grads_for(flips, member, stack, weights):
+def grads_for(flips, stack, weights):
     return pl.pallas_call(
         functools.partial(grad_kernel, flips),
         out_shape=[jax.ShapeDtypeStruct((PIXELS, 512), BF16)] * len(flips),
-        in_specs=[pl.BlockSpec(memory_space=pltpu.SMEM)]
-        + [pl.BlockSpec(memory_space=pltpu.VMEM)] * 2,
+        in_specs=[pl.BlockSpec(memory_space=pltpu.VMEM)] * 2,
         out_specs=[pl.BlockSpec(memory_space=pltpu.VMEM)] * len(flips),
         compiler_params=pltpu.CompilerParams(vmem_limit_bytes=18 * 2**20),
         cost_estimate=pl.CostEstimate(
             flops=2 * PIXELS * 28 * W * 512 * len(flips), bytes_accessed=10**6, transcendentals=0
         ),
         name="grads_for",
-    )(member, stack, weights)
-
-
-def last_kernel(a, b, c, order_t, out):
+    )(stack, weights)
+
+
+def last_kernel(a, b, c, out):
     total = a[...].astype(F32) + b[...].astype(F32) + c[...].astype(F32)
 
     def put(at, value):
         out[at : at + 192, :] = value
 
-    from_blocks(order_t[...], total.astype(BF16), put)
-
-
-def last_sum(a, b, c, order_t):
+    from_blocks(order_matrix(True), total.astype(BF16), put)
+
+
+def last_sum(a, b, c):
     return pl.pallas_call(
         last_kernel,
         out_shape=jax.ShapeDtypeStruct((PIXELS, 512), BF16),
-        in_specs=[pl.BlockSpec(memory_space=pltpu.VMEM)] * 4,
+        in_specs=[pl.BlockSpec(memory_space=pltpu.VMEM)] * 3,
         out_specs=pl.BlockSpec(memory_space=pltpu.VMEM),
         compiler_params=pltpu.CompilerParams(vmem_limit_bytes=10 * 2**20),
         name="last_sum",
-    )(a, b, c, order_t)
+    )(a, b, c)
 
 
 def flipped(x, bit):
@@ -550,46 +556,37 @@
 def on_device(
     features, point_weight, dilated_weight, branch_bias, project_weight, project_bias, cotangent
 ):
-    row = lax.axis_index("rows").astype(jnp.int32).reshape(1)
-    member = lax.axis_index("filt").astype(jnp.int32).reshape(1)
-    order = jnp.asarray(order_matrix(), BF16)
-    order_t = jnp.asarray(order_matrix().T, BF16)
     flat = features.reshape(PIXELS, CHANNELS)
     dilated = jnp.transpose(dilated_weight, (0, 1, 2, 4, 3)).reshape(27, W, CHANNELS)
     point = point_weight.T
-    bias = branch_bias.reshape(1, 4 * W)
     flat, dilated, point = (
         pltpu.with_memory_space_constraint(x, pltpu.HBM) for x in (flat, dilated, point)
     )
-    *sums, ordered, weights = odd_sums(row, flat, dilated, point, order)
+    *sums, ordered, weights = odd_sums(flat, dilated, point)
     received = [swapped(sums[n], SWAPS[n]) for n in range(4)]
-    sums = even_sums(row, ordered, weights)
+    sums = even_sums(ordered, weights, received[0])
     received += [swapped(sums[n], SWAPS[4 + n]) for n in range(2)]
-    own = own_sums(ordered, weights, bias)
-    acts = activations_of(row, own, received)
+    own = own_sums(ordered, weights, branch_bias)
+    acts = activations_of(own, received)
     across = flipped(acts, 2)
     beside = flipped(acts, 1)
     corner = flipped(across, 1)
     head_output, grads, *sends = head(
-        row,
-        member,
         (acts, beside, across, corner),
         project_weight,
         project_bias.reshape(1, 256),
         cotangent.reshape(PIXELS, 256),
-        order,
-        order_t,
-    )
-    arrived = [swapped(sends[n], x) for n, x in enumerate(SWAPS)]
-    stack = spread(row, grads, arrived)
-    near, far = grads_for((1, 3), member, stack, weights)
+    )
+    arrived = [swapped(sends[n], x) for n, x in enumerate(GRAD_SWAPS)]
+    stack = spread(grads, arrived)
+    near, far = grads_for((1, 3), stack, weights)
     near, far = flipped(near, 1), flipped(far, 1)
-    (kept,) = grads_for((2,), member, stack, weights)
+    (kept,) = grads_for((2,), stack, weights)
     crossing = (far.astype(F32) + kept.astype(F32)).astype(BF16)
     crossed = flipped(crossing, 2)
-    later, crossing = lax.optimization_barrier((member, crossing))
-    (kept,) = grads_for((0,), later, stack, weights)
-    feature_grad = last_sum(kept, near, crossed, order_t)
+    later, crossing = lax.optimization_barrier((stack, crossing))
+    (kept,) = grads_for((0,), later, weights)
+    feature_grad = last_sum(kept, near, crossed)
     return head_output.reshape(12, 48, W), feature_grad.reshape(12, 48, 512)
 
 

time: 93.3 us -> 79.9 us (0.86)
  the two profiles are of different devices: /device:TPU:2 before, /device:TPU:0 now
where the time goes in v1:
time: 79.9 us; the launch traced here: 79.6 us
  starting transfers between devices  35.1 us (44%)
  waiting for transfers between devices  25.3 us (32%)
  Pallas kernels  18.2 us (23%)
  between operations  0.84 us (1%)
    ppermute x12, starting transfers between devices, swapped(): return lax.ppermute(x, 'rows', pairs)  31.3 us
    ppermute x6, waiting for transfers between devices, flipped(): lax.ppermute(x, 'filt', [(i, i ^ bit) for i in range(lax.axis_size('filt'...  19.6 us
    pallas_call x1, Pallas kernels, odd_sums(): pl.pallas_call(odd_kernel, out_shape=[jax.ShapeDtypeStruct((HALF, 128), F...  6.03 us
    ppermute x12, waiting for transfers between devices, swapped(): return lax.ppermute(x, 'rows', pairs)  5.68 us
    pallas_call x3, Pallas kernels, grads_for(): pl.pallas_call(functools.partial(grad_kernel, flips), out_shape=[jax.Shap...  4.77 us
    ppermute x6, starting transfers between devices, flipped(): lax.ppermute(x, 'filt', [(i, i ^ bit) for i in range(lax.axis_size('filt'...  3.76 us
    pallas_call x1, Pallas kernels, head(): pl.pallas_call(head_kernel, out_shape=[jax.ShapeDtypeStruct((PIXELS, W),...  2.03 us
    pallas_call x1, Pallas kernels, own_sums(): pl.pallas_call(own_kernel, out_shape=jax.ShapeDtypeStruct((PIXELS, 4 * W)...  1.74 us
  transfers between devices with their start and end apart: 18, of which 7 were waited for; matrix products, arithmetic and copies ran while one was open for 0% of the time, Pallas kernels for 7%

profile of v1, /device:TPU:0, one launch (start us, length us, event | category | flops | bytes accessed | tf_op | source)
XLA Modules:
  0.0 79.6 jit_solution(3870450448199093892)
XLA Ops:
  0.6 6.0 %odd_sums.1 = (f32[288,128]{1,0:T(8,128)S(1)}, f32[288,128]{1,0:T(8,128)S(1)}, f32[288,128]{1,0:T(8,128)S(1)}, f32[288,128]{1,0:T(8,128)S(1)}, bf16[576,2048]{1,...) custom-call(bf16[576,2048]{1,0:T(8,128)(2,1)} %bitcast.12, bf16[27,64,2048]{2,1,0:T(8,128)(2,1)} %bitcast.11, ...), custom_call_target="tpu_custom_call" | custom-call | tf_op jit(solution)/shard_map/odd_sums/pallas_call | solution.py:274
  6.7 0.7 collective-permute-start
  7.3 0.7 collective-permute-start.1
  8.0 9.3 %collective-permute-start.2 = (f32[288,128]{1,0:T(8,128)S(1)}, f32[288,128]{1,0:T(8,128)S(1)}, u32[]{:S(2)}, u32[]{:S(2)}) collective-permute-start(f32[288,128]{1,0:T(8,128)S(1)} %get-tuple-element.25), channel_id=1, source_target_pairs={{0,12},{4,8},{8,4},{12,0},{16,28},{20,24},{24,20},{28,16},{1,13},{... | collective-permute-start | bytes 442376 | tf_op jit(solution)/shard_map/ppermute | solution.py:553
  17.3 1.5 %even_sums.1 = (f32[288,128]{1,0:T(8,128)S(1)}, f32[288,128]{1,0:T(8,128)S(1)}) custom-call(bf16[576,2048]{1,0:T(8,128)(2,1)S(1)} %get-tuple-element.21.ordered, bf16[1792,2048]{1,0:T(8,128)(2,1)S(1)} %get-tuple-element.22.weights, f32[288,128]{1,0:T(8,128)S(1)} %collective-permute-done.refs_0_), custom_call_target="tpu_custom_call" | custom-call | flops 1000000 | bytes 10000 | tf_op jit(solution)/shard_map/even_sums/pallas_call | solution.py:307
  18.9 0.7 collective-permute-start.4
  19.6 5.8 %collective-permute-start.5 = (f32[288,128]{1,0:T(8,128)S(1)}, f32[288,128]{1,0:T(8,128)S(1)}, u32[]{:S(2)}, u32[]{:S(2)}) collective-permute-start(f32[288,128]{1,0:T(8,128)S(1)} %get-tuple-element.28), channel_id=1, source_target_pairs={{0,8},{4,12},{8,0},{12,4},{16,24},{20,28},{24,16},{28,20},{1,9},{5... | collective-permute-start | bytes 442376 | tf_op jit(solution)/shard_map/ppermute | solution.py:553
  25.4 1.7 %own_sums.1.own = f32[576,256]{1,0:T(8,128)S(1)} custom-call(bf16[576,2048]{1,0:T(8,128)(2,1)S(1)} %get-tuple-element.21.ordered, bf16[1792,2048]{1,0:T(8,128)(2,1)S(1)} %get-tuple-element.22.weights, f32[4,64]{1,0:T(4,128)S(1)} %copy-done.2), custom_call_target="tpu_custom_call" | custom-call | flops 1000000 | bytes 10000 | tf_op jit(solution)/shard_map/own_sums/pallas_call | solution.py:347
  27.2 1.3 %collective-permute-done.5.refs_5_ = f32[288,128]{1,0:T(8,128)S(1)} collective-permute-done((f32[288,128]{1,0:T(8,128)S(1)}, f32[288,128]{1,0:T(8,128)S(1)}, u32[]{:S(2)}, u32[]{:S(2)}) %collective-permute-start.5) | collective-permute-done | bytes 147488 | tf_op jit(solution)/shard_map/ppermute | solution.py:553
  28.5 0.3 activations.1.a0
  28.8 1.6 %collective-permute-start.7 = (bf16[576,256]{1,0:T(8,128)(2,1)S(1)}, bf16[576,256]{1,0:T(8,128)(2,1)S(1)}, u32[]{:S(2)}, u32[]{:S(2)}) collective-permute-start(bf16[576,256]{1,0:T(8,128)(2,1)S(1)} %activations.1.a0), channel_id=1, source_target_pairs={{0,2},{1,3},{2,0},{3,1},{4,6},{5,7},{6,4},{7,5},{8,10},{9,11},{10,... | collective-permute-start | bytes 884744 | tf_op jit(solution)/shard_map/ppermute | solution.py:548
  30.3 5.2 %collective-permute-done.7.a2 = bf16[576,256]{1,0:T(8,128)(2,1)S(1)} collective-permute-done((bf16[576,256]{1,0:T(8,128)(2,1)S(1)}, bf16[576,256]{1,0:T(8,128)(2,1)S(1)}, u32[]{:S(2)}, u32[]{:S(2)}) %collective-permute-start.7) | collective-permute-done | bytes 294944 | tf_op jit(solution)/shard_map/ppermute | solution.py:548
  35.5 1.6 %collective-permute-done.8.a3 = bf16[576,256]{1,0:T(8,128)(2,1)S(1)} collective-permute-done((bf16[576,256]{1,0:T(8,128)(2,1)S(1)}, bf16[576,256]{1,0:T(8,128)(2,1)S(1)}, u32[]{:S(2)}, u32[]{:S(2)}) %collective-permute-start.8) | collective-permute-done | bytes 294944 | tf_op jit(solution)/shard_map/ppermute | solution.py:548
  37.1 2.0 %head.1 = (bf16[576,64]{1,0:T(8,128)(2,1)}, bf16[576,256]{1,0:T(8,128)(2,1)S(1)}, bf16[288,128]{1,0:T(8,128)(2,1)S(1)}, bf16[288,128]{1,0:T(8,128)(2,1)S(1)}, bf...) custom-call(bf16[576,256]{1,0:T(8,128)(2,1)S(1)} %activations.1.a0, ...), custom_call_target="tpu_custom_call" | custom-call | tf_op jit(solution)/shard_map/head/pallas_call | solution.py:439
  39.2 0.7 collective-permute-start.10
  39.8 0.7 collective-permute-start.11
  40.5 8.9 %collective-permute-start.12 = (bf16[288,128]{1,0:T(8,128)(2,1)S(1)}, bf16[288,128]{1,0:T(8,128)(2,1)S(1)}, u32[]{:S(2)}, u32[]{:S(2)}) collective-permute-start(bf16[288,128]{1,0:T(8,128)(2,1)S(1)} %get-tuple-element.34), channel_id=1, source_target_pairs={{0,12},{4,8},{8,4},{12,0},{16,28},{20,24},{24,20},{28,16},{1,13},{... | collective-permute-start | bytes 221192 | tf_op jit(solution)/shard_map/ppermute | solution.py:553
  49.4 0.7 collective-permute-start.13
  50.1 3.3 %collective-permute-start.14 = (bf16[288,128]{1,0:T(8,128)(2,1)S(1)}, bf16[288,128]{1,0:T(8,128)(2,1)S(1)}, u32[]{:S(2)}, u32[]{:S(2)}) collective-permute-start(bf16[288,128]{1,0:T(8,128)(2,1)S(1)} %get-tuple-element.36), channel_id=1, source_target_pairs={{0,8},{4,12},{8,0},{12,4},{16,24},{20,28},{24,16},{28,20},{1,9},{5... | collective-permute-start | bytes 221192 | tf_op jit(solution)/shard_map/ppermute | solution.py:553
  53.5 2.3 %collective-permute-done.14.refs_5_ = bf16[288,128]{1,0:T(8,128)(2,1)S(1)} collective-permute-done((bf16[288,128]{1,0:T(8,128)(2,1)S(1)}, bf16[288,128]{1,0:T(8,128)(2,1)S(1)}, u32[]{:S(2)}, u32[]{:S(2)}) %collective-permute-start.14) | collective-permute-done | bytes 73760 | tf_op jit(solution)/shard_map/ppermute | solution.py:553
  55.8 2.0 %collective-permute-done.9.refs_0_ = bf16[288,128]{1,0:T(8,128)(2,1)S(1)} collective-permute-done((bf16[288,128]{1,0:T(8,128)(2,1)S(1)}, bf16[288,128]{1,0:T(8,128)(2,1)S(1)}, u32[]{:S(2)}, u32[]{:S(2)}) %collective-permute-start.9) | collective-permute-done | bytes 73760 | tf_op jit(solution)/shard_map/ppermute | solution.py:553
  57.8 0.6 spread.1.stack
  58.4 2.3 %grads_for.3 = (bf16[576,512]{1,0:T(8,128)(2,1)S(1)}, bf16[576,512]{1,0:T(8,128)(2,1)S(1)}) custom-call(bf16[576,1792]{1,0:T(8,128)(2,1)S(1)} %spread.1.stack, bf16[1792,2048]{1,0:T(8,128)(2,1)S(1)} %get-tuple-element.22.weights), custom_call_target="tpu_custom_call" | custom-call | flops 2113929216 | bytes 1000000 | tf_op jit(solution)/shard_map/grads_for/pallas_call | solution.py:514
  60.7 0.1 collective-permute-start.15
  60.8 0.5 collective-permute-start.16
  61.3 1.2 %grads_for.4 = bf16[576,512]{1,0:T(8,128)(2,1)S(1)} custom-call(bf16[576,1792]{1,0:T(8,128)(2,1)S(1)} %spread.1.stack, bf16[1792,2048]{1,0:T(8,128)(2,1)S(1)} %get-tuple-element.22.weights), custom_call_target="tpu_custom_call" | custom-call | flops 1056964608 | bytes 1000000 | tf_op jit(solution)/shard_map/grads_for/pallas_call | solution.py:514
  62.5 0.3 collective-permute-done.15
  62.8 0.2 add_convert_fusion
  62.9 1.6 %collective-permute-start.17 = (bf16[576,512]{1,0:T(8,128)(2,1)S(1)}, bf16[576,512]{1,0:T(8,128)(2,1)S(1)}, u32[]{:S(2)}, u32[]{:S(2)}) collective-permute-start(bf16[576,512]{1,0:T(8,128)(2,1)S(1)} %add_convert_fusion), channel_id=1, source_target_pairs={{0,2},{1,3},{2,0},{3,1},{4,6},{5,7},{6,4},{7,5},{8,10},{9,11},{10,... | collective-permute-start | bytes 1769480 | tf_op jit(solution)/shard_map/ppermute | solution.py:548
  64.5 1.2 %grads_for.5.a = bf16[576,512]{1,0:T(8,128)(2,1)S(1)} custom-call(bf16[576,1792]{1,0:T(8,128)(2,1)S(1)} %spread.1.stack, bf16[1792,2048]{1,0:T(8,128)(2,1)S(1)} %get-tuple-element.22.weights), custom_call_target="tpu_custom_call" | custom-call | flops 1056964608 | bytes 1000000 | tf_op jit(solution)/shard_map/grads_for/pallas_call | solution.py:514
  65.8 12.6 %collective-permute-done.17.c = bf16[576,512]{1,0:T(8,128)(2,1)S(1)} collective-permute-done((bf16[576,512]{1,0:T(8,128)(2,1)S(1)}, bf16[576,512]{1,0:T(8,128)(2,1)S(1)}, u32[]{:S(2)}, u32[]{:S(2)}) %collective-permute-start.17) | collective-permute-done | bytes 589856 | tf_op jit(solution)/shard_map/ppermute | solution.py:548
  78.4 1.3 %last_sum.1 = bf16[576,512]{1,0:T(8,128)(2,1)} custom-call(bf16[576,512]{1,0:T(8,128)(2,1)S(1)} %grads_for.5.a, bf16[576,512]{1,0:T(8,128)(2,1)S(1)} %collective-permute-done.16.b, bf16[576,512]{1,0:T(8,128)(2,1)S(1)} %collective-permute-done.17.c), custom_call_target="tpu_custom_call" | custom-call | tf_op jit(solution)/shard_map/last_sum/pallas_call | solution.py:537
  (23 shorter events, 0.1 us)
Async XLA Ops:
  6.7 10.7 %collective-permute-start = (f32[288,128]{1,0:T(8,128)S(1)}, f32[288,128]{1,0:T(8,128)S(1)}, u32[]{:S(2)}, u32[]{:S(2)}) collective-permute-start(f32[288,128]{1,0:T(8,128)S(1)} %get-tuple-element.23), channel_id=1, source_target_pairs={{4,16},{12,24},{16,4},{24,12},{5,17},{13,25},{17,5},{25,13},{6,18}... | collective-permute-start | bytes 442376 | tf_op jit(solution)/shard_map/ppermute | solution.py:553
  7.3 19.8 %collective-permute-start.1 = (f32[288,128]{1,0:T(8,128)S(1)}, f32[288,128]{1,0:T(8,128)S(1)}, u32[]{:S(2)}, u32[]{:S(2)}) collective-permute-start(f32[288,128]{1,0:T(8,128)S(1)} %get-tuple-element.24), channel_id=1, source_target_pairs={{8,20},{12,16},{16,12},{20,8},{9,21},{13,17},{17,13},{21,9},{10,22... | collective-permute-start | bytes 442376 | tf_op jit(solution)/shard_map/ppermute | solution.py:553
  8.0 19.1 %collective-permute-start.2 = (f32[288,128]{1,0:T(8,128)S(1)}, f32[288,128]{1,0:T(8,128)S(1)}, u32[]{:S(2)}, u32[]{:S(2)}) collective-permute-start(f32[288,128]{1,0:T(8,128)S(1)} %get-tuple-element.25), channel_id=1, source_target_pairs={{0,12},{4,8},{8,4},{12,0},{16,28},{20,24},{24,20},{28,16},{1,13},{... | collective-permute-start | bytes 442376 | tf_op jit(solution)/shard_map/ppermute | solution.py:553
  17.3 9.8 %collective-permute-start.3 = (f32[288,128]{1,0:T(8,128)S(1)}, f32[288,128]{1,0:T(8,128)S(1)}, u32[]{:S(2)}, u32[]{:S(2)}) collective-permute-start(f32[288,128]{1,0:T(8,128)S(1)} %get-tuple-element.26), channel_id=1, source_target_pairs={{0,4},{4,0},{8,12},{12,8},{16,20},{20,16},{24,28},{28,24},{1,5},{5... | collective-permute-start | bytes 442376 | tf_op jit(solution)/shard_map/ppermute | solution.py:553
  17.3 8.0 %copy-start.2 = (f32[4,64]{1,0:T(4,128)S(1)}, f32[4,64]{1,0:T(4,128)}, u32[]{:S(2)}) copy-start(f32[4,64]{1,0:T(4,128)} %bias.1) | copy-start | bytes 3076
  18.9 8.3 %collective-permute-start.4 = (f32[288,128]{1,0:T(8,128)S(1)}, f32[288,128]{1,0:T(8,128)S(1)}, u32[]{:S(2)}, u32[]{:S(2)}) collective-permute-start(f32[288,128]{1,0:T(8,128)S(1)} %get-tuple-element.27), channel_id=1, source_target_pairs={{8,16},{12,20},{16,8},{20,12},{9,17},{13,21},{17,9},{21,13},{10,18... | collective-permute-start | bytes 442376 | tf_op jit(solution)/shard_map/ppermute | solution.py:553
  19.6 17.6 %copy-start = (bf16[4,256,256]{2,1,0:T(8,128)(2,1)S(1)}, bf16[4,256,256]{2,1,0:T(8,128)(2,1)}, u32[]{:S(2)}) copy-start(bf16[4,256,256]{2,1,0:T(8,128)(2,1)} %project.1) | copy-start | bytes 1572868
  19.6 17.6 %copy-start.1 = (bf16[12,48,256]{2,1,0:T(8,128)(2,1)S(1)}, bf16[12,48,256]{2,1,0:T(8,128)(2,1)}, u32[]{:S(2)}) copy-start(bf16[12,48,256]{2,1,0:T(8,128)(2,1)} %param.13) | copy-start | bytes 884740
  19.6 17.5 %copy-start.3 = (f32[256]{0:T(256)S(1)}, f32[256]{0:T(256)}, u32[]{:S(2)}) copy-start(f32[256]{0:T(256)} %param.12) | copy-start | bytes 3076
  19.6 8.9 %collective-permute-start.5 = (f32[288,128]{1,0:T(8,128)S(1)}, f32[288,128]{1,0:T(8,128)S(1)}, u32[]{:S(2)}, u32[]{:S(2)}) collective-permute-start(f32[288,128]{1,0:T(8,128)S(1)} %get-tuple-element.28), channel_id=1, source_target_pairs={{0,8},{4,12},{8,0},{12,4},{16,24},{20,28},{24,16},{28,20},{1,9},{5... | collective-permute-start | bytes 442376 | tf_op jit(solution)/shard_map/ppermute | solution.py:553
  28.8 6.8 %collective-permute-start.7 = (bf16[576,256]{1,0:T(8,128)(2,1)S(1)}, bf16[576,256]{1,0:T(8,128)(2,1)S(1)}, u32[]{:S(2)}, u32[]{:S(2)}) collective-permute-start(bf16[576,256]{1,0:T(8,128)(2,1)S(1)} %activations.1.a0), channel_id=1, source_target_pairs={{0,2},{1,3},{2,0},{3,1},{4,6},{5,7},{6,4},{7,5},{8,10},{9,11},{10,... | collective-permute-start | bytes 884744 | tf_op jit(solution)/shard_map/ppermute | solution.py:548
  30.3 5.2 %collective-permute-start.6 = (bf16[576,256]{1,0:T(8,128)(2,1)S(1)}, bf16[576,256]{1,0:T(8,128)(2,1)S(1)}, u32[]{:S(2)}, u32[]{:S(2)}) collective-permute-start(bf16[576,256]{1,0:T(8,128)(2,1)S(1)} %activations.1.a0), channel_id=1, source_target_pairs={{0,1},{1,0},{2,3},{3,2},{4,5},{5,4},{6,7},{7,6},{8,9},{9,8},{10,11... | collective-permute-start | bytes 884744 | tf_op jit(solution)/shard_map/ppermute | solution.py:548
  35.5 1.6 %collective-permute-start.8 = (bf16[576,256]{1,0:T(8,128)(2,1)S(1)}, bf16[576,256]{1,0:T(8,128)(2,1)S(1)}, u32[]{:S(2)}, u32[]{:S(2)}) collective-permute-start(bf16[576,256]{1,0:T(8,128)(2,1)S(1)} %collective-permute-done.7.a2), channel_id=1, source_target_pairs={{0,1},{1,0},{2,3},{3,2},{4,5},{5,4},{6,7},{7,6},{8,9},{9,8},{10,11... | collective-permute-start | bytes 884744 | tf_op jit(solution)/shard_map/ppermute | solution.py:548
  39.2 14.3 %collective-permute-start.10 = (bf16[288,128]{1,0:T(8,128)(2,1)S(1)}, bf16[288,128]{1,0:T(8,128)(2,1)S(1)}, u32[]{:S(2)}, u32[]{:S(2)}) collective-permute-start(bf16[288,128]{1,0:T(8,128)(2,1)S(1)} %get-tuple-element.32), channel_id=1, source_target_pairs={{4,16},{12,24},{16,4},{24,12},{5,17},{13,25},{17,5},{25,13},{6,18}... | collective-permute-start | bytes 221192 | tf_op jit(solution)/shard_map/ppermute | solution.py:553
  39.8 13.6 %collective-permute-start.11 = (bf16[288,128]{1,0:T(8,128)(2,1)S(1)}, bf16[288,128]{1,0:T(8,128)(2,1)S(1)}, u32[]{:S(2)}, u32[]{:S(2)}) collective-permute-start(bf16[288,128]{1,0:T(8,128)(2,1)S(1)} %get-tuple-element.33), channel_id=1, source_target_pairs={{8,20},{12,16},{16,12},{20,8},{9,21},{13,17},{17,13},{21,9},{10,22... | collective-permute-start | bytes 221192 | tf_op jit(solution)/shard_map/ppermute | solution.py:553
  40.5 12.9 %collective-permute-start.12 = (bf16[288,128]{1,0:T(8,128)(2,1)S(1)}, bf16[288,128]{1,0:T(8,128)(2,1)S(1)}, u32[]{:S(2)}, u32[]{:S(2)}) collective-permute-start(bf16[288,128]{1,0:T(8,128)(2,1)S(1)} %get-tuple-element.34), channel_id=1, source_target_pairs={{0,12},{4,8},{8,4},{12,0},{16,28},{20,24},{24,20},{28,16},{1,13},{... | collective-permute-start | bytes 221192 | tf_op jit(solution)/shard_map/ppermute | solution.py:553
  49.4 4.0 %collective-permute-start.13 = (bf16[288,128]{1,0:T(8,128)(2,1)S(1)}, bf16[288,128]{1,0:T(8,128)(2,1)S(1)}, u32[]{:S(2)}, u32[]{:S(2)}) collective-permute-start(bf16[288,128]{1,0:T(8,128)(2,1)S(1)} %get-tuple-element.35), channel_id=1, source_target_pairs={{8,16},{12,20},{16,8},{20,12},{9,17},{13,21},{17,9},{21,13},{10,18... | collective-permute-start | bytes 221192 | tf_op jit(solution)/shard_map/ppermute | solution.py:553
  50.1 5.7 %collective-permute-start.14 = (bf16[288,128]{1,0:T(8,128)(2,1)S(1)}, bf16[288,128]{1,0:T(8,128)(2,1)S(1)}, u32[]{:S(2)}, u32[]{:S(2)}) collective-permute-start(bf16[288,128]{1,0:T(8,128)(2,1)S(1)} %get-tuple-element.36), channel_id=1, source_target_pairs={{0,8},{4,12},{8,0},{12,4},{16,24},{20,28},{24,16},{28,20},{1,9},{5... | collective-permute-start | bytes 221192 | tf_op jit(solution)/shard_map/ppermute | solution.py:553
  53.4 4.4 %collective-permute-start.9 = (bf16[288,128]{1,0:T(8,128)(2,1)S(1)}, bf16[288,128]{1,0:T(8,128)(2,1)S(1)}, u32[]{:S(2)}, u32[]{:S(2)}) collective-permute-start(bf16[288,128]{1,0:T(8,128)(2,1)S(1)} %get-tuple-element.31), channel_id=1, source_target_pairs={{0,4},{4,0},{8,12},{12,8},{16,20},{20,16},{24,28},{28,24},{1,5},{5... | collective-permute-start | bytes 221192 | tf_op jit(solution)/shard_map/ppermute | solution.py:553
  60.7 2.1 %collective-permute-start.15 = (bf16[576,512]{1,0:T(8,128)(2,1)S(1)}, bf16[576,512]{1,0:T(8,128)(2,1)S(1)}, u32[]{:S(2)}, u32[]{:S(2)}) collective-permute-start(bf16[576,512]{1,0:T(8,128)(2,1)S(1)} %get-tuple-element.37), channel_id=1, source_target_pairs={{0,1},{1,0},{2,3},{3,2},{4,5},{5,4},{6,7},{7,6},{8,9},{9,8},{10,11... | collective-permute-start | bytes 1769480 | tf_op jit(solution)/shard_map/ppermute | solution.py:548
  60.8 5.0 %collective-permute-start.16 = (bf16[576,512]{1,0:T(8,128)(2,1)S(1)}, bf16[576,512]{1,0:T(8,128)(2,1)S(1)}, u32[]{:S(2)}, u32[]{:S(2)}) collective-permute-start(bf16[576,512]{1,0:T(8,128)(2,1)S(1)} %get-tuple-element.39), channel_id=1, source_target_pairs={{0,1},{1,0},{2,3},{3,2},{4,5},{5,4},{6,7},{7,6},{8,9},{9,8},{10,11... | collective-permute-start | bytes 1769480 | tf_op jit(solution)/shard_map/ppermute | solution.py:548
  62.9 15.4 %collective-permute-start.17 = (bf16[576,512]{1,0:T(8,128)(2,1)S(1)}, bf16[576,512]{1,0:T(8,128)(2,1)S(1)}, u32[]{:S(2)}, u32[]{:S(2)}) collective-permute-start(bf16[576,512]{1,0:T(8,128)(2,1)S(1)} %add_convert_fusion), channel_id=1, source_target_pairs={{0,2},{1,3},{2,0},{3,1},{4,6},{5,7},{6,4},{7,5},{8,10},{9,11},{10,... | collective-permute-start | bytes 1769480 | tf_op jit(solution)/shard_map/ppermute | solution.py:548
